TPU v7x, 512 devices: a whole 4x4x16 slice. The times are simulated.
512 devices in a mesh: ctx: 32 (over z, core), head: 16 (over x, y).
Axes of the slice: x: 4, y: 4, z: 16, core: 2. Of those that a mesh axis runs over, the one named last changes fastest.
Arguments:
- q_nope: bfloat16 [4096, 8192], P('ctx', 'head'), may hold values from -6 to 6
- q_rope: bfloat16 [4096, 4096], P('ctx', 'head'), may hold values from -80 to 80
- kv_cache: bfloat16 [4096, 576], P('ctx'), may hold values from -180 to 180
- kv_gain: bfloat16 [512], replicated, may hold values from 0.099609375 to 1.8984375
- w_uk: bfloat16 [64, 128, 512], P('head'), may hold values from -0.5 to 0.5
- w_uv: bfloat16 [64, 512, 128], P('head'), may hold values from -0.25 to 0.25
- attn_out: bfloat16 [4096, 8192], P('ctx', 'head'), may hold values from -6 to 6
- d_out: bfloat16 [4096, 8192], P('ctx', 'head'), may hold values from -6 to 6
- span_table: int32 [32, 2], replicated, may hold values from 0 to 63, as said below
Outputs:
- d_q_nope: bfloat16 [4096, 8192], P('ctx', 'head')
- d_q_rope: bfloat16 [4096, 4096], P('ctx', 'head')
- d_cache: float32 [4096, 576], P('ctx')
Inputs may be any that keep to these rules, and one draw needn't show every extreme that they name: `span_table`: row d lists the two blocks of 64 positions held by the rows of ctx index d, in this order: a block c below 32, then its mirror 64 - 1 - c. The first column is a permutation.
All inputs are finite; a program needn't handle non-finite values.
Results may differ from a plain program's by a relative error of at most 0.02.
Values may be sent and summed in bfloat16 or wider, within the bound.
A program may use at most 64 MiB of HBM per device.

v0:
```python
import jax
import jax.numpy as jnp
from jax import lax
from jax.sharding import PartitionSpec as P

neg_big = -1e30
eps_norm = 1e-06


def latent_rows(raw_rows, gain_rows):
    values = raw_rows.astype(jnp.float32)
    inverse = lax.rsqrt(jnp.mean(values * values, axis=-1, keepdims=True) + eps_norm)
    return (
        values,
        inverse,
        (values * inverse * gain_rows.astype(jnp.float32)).astype(jnp.bfloat16),
    )


def norm_backward(grad_rows, raw_rows, gain_rows, lat_width):
    values, inverse, unused_rows = latent_rows(raw_rows[:, :lat_width], gain_rows)
    scaled = grad_rows[:, :lat_width] * gain_rows.astype(jnp.float32)
    inner_mean = jnp.mean(values * scaled, axis=-1, keepdims=True)
    d_raw = inverse * scaled - values * inverse * inverse * inverse * inner_mean
    return jnp.concatenate([d_raw, grad_rows[:, lat_width:]], axis=1)


def add_latent(full_terms, latent_terms):
    width = latent_terms.shape[-1]
    return jnp.concatenate(
        [full_terms[..., :width] + latent_terms, full_terms[..., width:]], axis=-1
    )


def local(q_nope, q_rope, kv_cache, kv_gain, w_uk, w_uv, attn_out, d_out, span_table):
    tok_rows = q_nope.shape[0]
    span_len = tok_rows // 2
    head_count = w_uk.shape[0]
    nope_width = w_uk.shape[1]
    lat_width = w_uk.shape[2]
    value_width = w_uv.shape[2]
    rope_width = q_rope.shape[1] // head_count
    row_count = span_len * head_count
    cat_width = lat_width + rope_width
    score_scale = float(nope_width + rope_width) ** (-0.5)
    ctx_count = lax.axis_size("ctx")
    my_index = lax.axis_index("ctx")
    my_spans = lax.dynamic_index_in_dim(span_table, my_index, 0, keepdims=False)
    nope_view = q_nope.reshape(2, span_len, head_count, nope_width)
    q_latent = jnp.einsum(
        "schn,hnl->schl", nope_view, w_uk, preferred_element_type=jnp.float32
    ).astype(jnp.bfloat16)
    rope_view = q_rope.reshape(2, span_len, head_count, rope_width)
    query_cat = jnp.concatenate([q_latent, rope_view], axis=3).reshape(2, row_count, cat_width)
    grad_view = d_out.reshape(2, span_len, head_count, value_width)
    d_latent = jnp.einsum("schv,hlv->schl", grad_view, w_uv, preferred_element_type=jnp.float32)
    d_latent = d_latent.astype(jnp.bfloat16).reshape(2, row_count, lat_width)
    out_view = attn_out.reshape(2, span_len, head_count, value_width)
    row_delta = jnp.sum(
        grad_view.astype(jnp.float32) * out_view.astype(jnp.float32), axis=3
    ).reshape(2, row_count)
    offsets = jnp.arange(span_len, dtype=jnp.int32)
    row_offsets = jnp.arange(row_count, dtype=jnp.int32) // head_count
    query_pos = my_spans[:, None] * span_len + row_offsets[None, :]
    gathered = lax.all_gather(kv_cache, "ctx", axis=0, tiled=True)
    latent_all = latent_rows(gathered[:, :lat_width], kv_gain)[2]
    key_cat = jnp.concatenate([latent_all, gathered[:, lat_width:]], axis=1).reshape(
        ctx_count, 2, span_len, cat_width
    )
    upper_all = span_table[:, 0] > my_spans[0]

    def pair_scores(key_rows, key_table):
        upper_half = key_table[:, 0] > my_spans[0]
        first_keys = key_rows[:, 0]
        other_keys = jnp.where(upper_half[:, None, None], key_rows[:, 1], key_rows[:, 0])
        first_pos = key_table[:, 0][:, None] * span_len + offsets[None, :]
        other_pos = (
            jnp.where(upper_half, key_table[:, 1], key_table[:, 0])[:, None] * span_len
            + offsets[None, :]
        )
        picked_query = jnp.where(upper_half[:, None, None], query_cat[1][None], query_cat[0][None])
        picked_pos = jnp.where(upper_half[:, None], query_pos[1][None], query_pos[0][None])
        first_scores = (
            jnp.einsum("gkd,rd->gkr", first_keys, query_cat[1], preferred_element_type=jnp.float32)
            * score_scale
        )
        other_scores = (
            jnp.einsum("gkd,grd->gkr", other_keys, picked_query, preferred_element_type=jnp.float32)
            * score_scale
        )
        first_scores = jnp.where(
            first_pos[:, :, None] <= query_pos[1][None, None, :], first_scores, neg_big
        )
        other_scores = jnp.where(
            other_pos[:, :, None] <= picked_pos[:, None, :], other_scores, neg_big
        )
        return (first_scores, other_scores)

    group_size = min(8, ctx_count)
    group_count = ctx_count // group_size
    key_groups = key_cat.reshape(group_count, group_size, 2, span_len, cat_width)
    table_groups = span_table.reshape(group_count, group_size, 2)
    first_all, other_all = lax.map(
        lambda group_item: pair_scores(group_item[0], group_item[1]), (key_groups, table_groups)
    )
    first_all = first_all.reshape(ctx_count, span_len, row_count)
    other_all = other_all.reshape(ctx_count, span_len, row_count)
    own_keys = lax.dynamic_index_in_dim(key_cat, my_index, 0, keepdims=False)[1]
    own_pos = my_spans[1] * span_len + offsets
    own_scores = (
        jnp.einsum("kd,rd->kr", own_keys, query_cat[1], preferred_element_type=jnp.float32)
        * score_scale
    )
    own_scores = jnp.where(own_pos[:, None] <= query_pos[1][None, :], own_scores, neg_big)
    other_max = jnp.max(other_all, axis=1)
    top_upper = jnp.maximum(jnp.max(first_all, axis=(0, 1)), jnp.max(own_scores, axis=0))
    top_upper = jnp.maximum(
        top_upper, jnp.max(jnp.where(upper_all[:, None], other_max, neg_big), axis=0)
    )
    top_lower = jnp.max(jnp.where(upper_all[:, None], neg_big, other_max), axis=0)
    row_top = jnp.where(upper_all[:, None], top_upper[None, :], top_lower[None, :])
    other_sum = jnp.sum(jnp.exp(other_all - row_top[:, None, :]), axis=1)
    upper_sum = jnp.sum(jnp.exp(first_all - top_upper[None, None, :]), axis=(0, 1))
    upper_sum = upper_sum + jnp.sum(jnp.exp(own_scores - top_upper[None, :]), axis=0)
    upper_sum = upper_sum + jnp.sum(jnp.where(upper_all[:, None], other_sum, 0.0), axis=0)
    lower_sum = jnp.sum(jnp.where(upper_all[:, None], 0.0, other_sum), axis=0)
    log_total = jnp.stack([top_lower + jnp.log(lower_sum), top_upper + jnp.log(upper_sum)])
    own_prob = jnp.exp(own_scores - log_total[1][None, :])
    own_dp = jnp.einsum(
        "kl,rl->kr", own_keys[:, :lat_width], d_latent[1], preferred_element_type=jnp.float32
    )
    own_ds = (own_prob * (own_dp - row_delta[1][None, :]) * score_scale).astype(jnp.bfloat16)
    own_dq = jnp.einsum("kr,kd->rd", own_ds, own_keys, preferred_element_type=jnp.float32)
    own_dk = add_latent(
        jnp.einsum("kr,rd->kd", own_ds, query_cat[1], preferred_element_type=jnp.float32),
        jnp.einsum(
            "kr,rl->kl",
            own_prob.astype(jnp.bfloat16),
            d_latent[1],
            preferred_element_type=jnp.float32,
        ),
    )

    def pair_grads(key_rows, key_table, first_scores, other_scores, owner_ids):
        upper_half = key_table[:, 0] > my_spans[0]
        first_keys = key_rows[:, 0]
        other_keys = jnp.where(upper_half[:, None, None], key_rows[:, 1], key_rows[:, 0])
        picked_query = jnp.where(upper_half[:, None, None], query_cat[1][None], query_cat[0][None])
        picked_grad = jnp.where(upper_half[:, None, None], d_latent[1][None], d_latent[0][None])
        picked_delta = jnp.where(upper_half[:, None], row_delta[1][None], row_delta[0][None])
        picked_log = jnp.where(upper_half[:, None], log_total[1][None], log_total[0][None])
        first_prob = jnp.exp(first_scores - log_total[1][None, None, :])
        other_prob = jnp.exp(other_scores - picked_log[:, None, :])
        first_dp = jnp.einsum(
            "gkl,rl->gkr",
            first_keys[..., :lat_width],
            d_latent[1],
            preferred_element_type=jnp.float32,
        )
        other_dp = jnp.einsum(
            "gkl,grl->gkr",
            other_keys[..., :lat_width],
            picked_grad,
            preferred_element_type=jnp.float32,
        )
        first_ds = (first_prob * (first_dp - row_delta[1][None, None, :]) * score_scale).astype(
            jnp.bfloat16
        )
        other_ds = (other_prob * (other_dp - picked_delta[:, None, :]) * score_scale).astype(
            jnp.bfloat16
        )
        first_dq = jnp.einsum(
            "gkr,gkd->rd", first_ds, first_keys, preferred_element_type=jnp.float32
        )
        other_dq = jnp.einsum(
            "gkr,gkd->grd", other_ds, other_keys, preferred_element_type=jnp.float32
        )
        lower_dq = jnp.sum(jnp.where(upper_half[:, None, None], 0.0, other_dq), axis=0)
        upper_dq = jnp.sum(jnp.where(upper_half[:, None, None], other_dq, 0.0), axis=0) + first_dq
        first_dk = add_latent(
            jnp.einsum("gkr,rd->gkd", first_ds, query_cat[1], preferred_element_type=jnp.float32),
            jnp.einsum(
                "gkr,rl->gkl",
                first_prob.astype(jnp.bfloat16),
                d_latent[1],
                preferred_element_type=jnp.float32,
            ),
        )
        other_dk = add_latent(
            jnp.einsum("gkr,grd->gkd", other_ds, picked_query, preferred_element_type=jnp.float32),
            jnp.einsum(
                "gkr,grl->gkl",
                other_prob.astype(jnp.bfloat16),
                picked_grad,
                preferred_element_type=jnp.float32,
            ),
        )
        lower_rows = first_dk + jnp.where(upper_half[:, None, None], 0.0, other_dk)
        upper_rows = jnp.where(upper_half[:, None, None], other_dk, 0.0)
        upper_rows = upper_rows + jnp.where(
            (owner_ids == my_index)[:, None, None], own_dk[None], 0.0
        )
        owner_terms = jnp.concatenate([lower_rows, upper_rows], axis=1).astype(jnp.bfloat16)
        return (jnp.stack([lower_dq, upper_dq]), owner_terms)

    zero_dq = jnp.zeros((2, row_count, cat_width), jnp.float32)
    first_groups = first_all.reshape(group_count, group_size, span_len, row_count)
    other_groups = other_all.reshape(group_count, group_size, span_len, row_count)
    owner_groups = jnp.arange(ctx_count, dtype=jnp.int32).reshape(group_count, group_size)

    def group_step(dq_carry, group_item):
        dq_part, owner_terms = pair_grads(*group_item)
        return (dq_carry + dq_part, owner_terms)

    dq_sum, owner_terms = lax.scan(
        group_step, zero_dq, (key_groups, table_groups, first_groups, other_groups, owner_groups)
    )
    dq_total, owner_terms = (dq_sum, owner_terms.reshape(ctx_count, tok_rows, cat_width))
    received = lax.all_to_all(owner_terms, "ctx", split_axis=0, concat_axis=0, tiled=True)
    key_grads = jnp.sum(received.astype(jnp.float32), axis=0)
    summed = lax.psum(key_grads.astype(jnp.bfloat16), "head").astype(jnp.float32)
    d_cache = norm_backward(summed, kv_cache, kv_gain, lat_width)
    dq_total = dq_total + jnp.stack([jnp.zeros_like(own_dq), own_dq])
    dq_latent = (
        dq_total[..., :lat_width].astype(jnp.bfloat16).reshape(2, span_len, head_count, lat_width)
    )
    d_q_nope = jnp.einsum("schl,hnl->schn", dq_latent, w_uk, preferred_element_type=jnp.float32)
    d_q_nope = d_q_nope.astype(jnp.bfloat16).reshape(tok_rows, head_count * nope_width)
    d_q_rope = (
        dq_total[..., lat_width:].astype(jnp.bfloat16).reshape(tok_rows, head_count * rope_width)
    )
    return (d_q_nope, d_q_rope, d_cache)


def solution(mesh):
    in_specs = (
        P("ctx", "head"),
        P("ctx", "head"),
        P("ctx", None),
        P(),
        P("head", None, None),
        P("head", None, None),
        P("ctx", "head"),
        P("ctx", "head"),
        P(),
    )
    out_specs = (P("ctx", "head"), P("ctx", "head"), P("ctx", None))
    return jax.shard_map(local, mesh=mesh, in_specs=in_specs, out_specs=out_specs, check_vma=False)
```

profile of v0, /device:TPU:1, one launch (start us, length us, event | category | flops | bytes accessed | tf_op | source)
XLA Modules:
  0.0 527.5 jit_solution(8354804672283491970)
XLA Ops:
  7.2 1.8 copy.37
  9.1 1.0 reshape.520
  10.0 1.0 concatenate.60
  11.0 0.9 reshape.521
  12.0 1.0 reshape.531
  13.7 1.3 copy.47
  20.5 1.1 copy.43
  21.9 0.9 squeeze.81
  25.7 66.0 %all-gather.2.cloned.1.call-done = bf16[4096,576]{1,0:T(8,128)(2,1)} async-done(((bf16[128,576]{1,0:T(8,128)(2,1)}), bf16[4096,576]{1,0:T(8,128)(2,1)}) %all-gather.2.cloned.1.call-update) | async-done | bytes 4718608 | tf_op jit(solution)/shard_map/all_gather | solution.py:65
  91.7 3.2 fusion.89
  95.4 1.1 fusion.91
  97.2 3.3 copy.42
  101.2 17.5 %while.27 = (s32[]{:T(128)}, f32[4,8,64,256]{3,2,1,0:T(8,128)}, f32[4,8,64,256]{3,2,1,0:T(8,128)}, s32[4,8,2]{1,2,0:T(2,128)S(1)}, s32[2,256]{1,0:T(2,128)S(1)},...) while((s32[]{:T(128)}, f32[4,8,64,256]{3,2,1,0:T(8,128)}, ...), condition=%wide.region_2.3_spmd.clone.clone, body=%wide.region_1.2_spmd.clone.clone.sunk | while | flops 304253984 | bytes 7475693 | solution.py:103
  101.5 1.4 dynamic-slice_bitcast_fusion.5
  103.0 1.5 fusion.174
  104.4 1.2 fusion.173
  105.9 1.4 dynamic-slice_bitcast_fusion.5
  107.4 1.5 fusion.174
  108.8 1.2 fusion.173
  110.3 1.4 dynamic-slice_bitcast_fusion.5
  111.7 1.5 fusion.174
  113.2 1.2 fusion.173
  114.7 1.4 dynamic-slice_bitcast_fusion.5
  116.1 1.5 fusion.174
  117.5 1.2 fusion.173
  118.7 1.9 reduce_max.45
  120.7 1.8 reduce_max.47
  122.5 0.9 dynamic-slice_bitcast_fusion.2
  123.9 3.0 exponential_reduce_fusion
  128.3 60.8 %while.28 = (s32[]{:T(128)}, f32[2,256,576]{1,2,0:T(8,128)}, bf16[4,8,128,576]{2,3,1,0:T(8,128)(2,1)}, s32[4,8,2]{1,2,0:T(2,128)S(1)}, s32[2]{0:T(128)}, /*index...) while((s32[]{:T(128)}, f32[2,256,576]{1,2,0:T(8,128)}, ...), condition=%wide.region_17.18_spmd.clone, body=%wide.region_14.17_spmd.clone.sunk | while | flops 1157255168 | bytes 66949796 | solution.py:215
  129.7 1.6 dynamic-slice_bitcast_fusion.6
  131.7 0.9 fusion.193
  132.5 1.1 select_reduce_fusion.7
  133.6 0.9 fusion.196
  135.6 0.9 copy-done.4
  137.3 1.2 maximum_add_fusion.3
  141.3 1.1 constant_dynamic-update-slice_fusion.2
  143.9 1.6 dynamic-slice_bitcast_fusion.6
  146.8 1.1 select_reduce_fusion.7
  147.8 0.9 fusion.196
  149.9 0.9 copy-done.4
  151.5 2.5 maximum_add_fusion.3
  156.8 1.1 constant_dynamic-update-slice_fusion.2
  159.4 1.6 dynamic-slice_bitcast_fusion.6
  161.4 0.9 fusion.193
  162.3 1.1 select_reduce_fusion.7
  163.4 0.9 fusion.196
  165.4 0.9 copy-done.4
  167.0 2.5 maximum_add_fusion.3
  172.3 1.2 constant_dynamic-update-slice_fusion.2
  174.9 1.6 dynamic-slice_bitcast_fusion.6
  176.9 0.9 fusion.193
  177.8 1.1 select_reduce_fusion.7
  178.9 0.9 fusion.196
  180.9 0.9 copy-done.4
  182.5 2.5 maximum_add_fusion.3
  187.8 1.1 constant_dynamic-update-slice_fusion.2
  189.0 7.9 %all-to-all-start = ((bf16[32,128,576]{1,2,0:T(8,128)(2,1)}), bf16[32,128,576]{1,2,0:T(8,128)(2,1)}, u32[]{:S(2)}, u32[]{:S(2)}) async-start(bf16[32,128,576]{1,2,0:T(8,128)(2,1)} %bitcast.265), calls=%async_computation | async-start | bytes 9437184 | tf_op jit(solution)/shard_map/all_to_all | solution.py:219
  197.3 1.4 add_convert_fusion.1
  199.3 202.3 %all-to-all-done = bf16[32,128,576]{1,2,0:T(8,128)(2,1)} async-done(((bf16[32,128,576]{1,2,0:T(8,128)(2,1)}), bf16[32,128,576]{1,2,0:T(8,128)(2,1)}, u32[]{:S(2)}, u32[]{:S(2)}) %all-to-all-start) | async-done | bytes 4718624 | tf_op jit(solution)/shard_map/all_to_all | solution.py:219
  401.6 3.0 reduce_sum.119
  407.5 110.3 %all-reduce.3.cloned.1.call-done = bf16[128,576]{1,0:T(8,128)(2,1)} async-done(((bf16[128,576]{1,0:T(8,128)(2,1)}), bf16[128,576]{1,0:T(8,128)(2,1)}) %all-reduce.3.cloned.1.call-update) | async-done | bytes 147472 | tf_op jit(solution)/shard_map/psum | solution.py:221
  517.8 0.9 convert_element_type.91
  519.8 0.9 copy.60
  (275 shorter events, 44.6 us)
Async XLA Ops:
  7.2 11.7 %copy-start = (bf16[4,128,512]{2,1,0:T(8,128)(2,1)S(1)}, bf16[4,128,512]{2,1,0:T(8,128)(2,1)}, u32[]{:S(2)}) copy-start(bf16[4,128,512]{2,1,0:T(8,128)(2,1)} %param.17) | copy-start | bytes 1572868
  7.2 6.1 %copy-start.16 = (bf16[4,512,128]{2,1,0:T(8,128)(2,1)S(1)}, bf16[4,512,128]{2,1,0:T(8,128)(2,1)}, u32[]{:S(2)}) copy-start(bf16[4,512,128]{2,1,0:T(8,128)(2,1)} %param.18) | copy-start | bytes 1572868
  7.2 84.5 %all-gather.2.cloned.1.call-start = ((), (), s32[]{:S(2)}) async-start(), calls=%async_computation.1 | async-start | bytes 5406720 | tf_op jit(solution)/shard_map/all_gather | solution.py:65
  13.3 1.8 copy-start.26
  13.3 4.6 copy-start.27
  13.3 4.6 copy-start.19
  13.7 5.4 %copy-start.9 = (bf16[2,64,4,512]{3,1,0,2:T(8,128)(2,1)}, bf16[2,64,4,512]{3,1,0,2:T(8,128)(2,1)S(1)}, u32[]{:S(2)}) copy-start(bf16[2,64,4,512]{3,1,0,2:T(8,128)(2,1)S(1)} %convert_bitcast_fusion) | copy-start | bytes 1572868
  17.9 77.0 %copy-start.20 = (f32[512]{0:T(512)}, f32[512]{0:T(512)S(1)}, u32[]{:S(2)}) copy-start(f32[512]{0:T(512)S(1)} %convert_element_type.77) | copy-start | bytes 6148
  20.5 2.4 slice-start.2
  21.5 1.2 copy-start.13
  91.6 3.7 copy-start.6
  95.4 1.2 slice-start.1
  97.2 4.0 copy-start.5
  118.7 8.9 %copy-start.22 = (s32[2]{0:T(128)}, s32[2]{0:T(128)S(1)}, u32[]{:S(2)}) copy-start(s32[2]{0:T(128)S(1)} %get-tuple-element.691) | copy-start | bytes 28
  118.7 4.6 copy-start.23
  118.7 4.8 copy-start.10
  118.7 4.8 copy-start.25
  118.7 4.8 copy-start.28
  123.4 3.6 copy-start.14
  123.9 3.1 copy-start.11
  123.9 3.1 copy-start.24
  127.2 1.1 copy-start.17
  128.3 10.2 %copy-start.1 = (bf16[2,256,576]{1,2,0:T(8,128)(2,1)}, bf16[2,256,576]{1,2,0:T(8,128)(2,1)S(1)}, u32[]{:S(2)}) copy-start(bf16[2,256,576]{1,2,0:T(8,128)(2,1)S(1)} %get-tuple-element.672) | copy-start | bytes 1769476 | tf_op jit(solution)/shard_map/while
  129.7 2.0 copy-start.7
  134.5 1.1 copy-start.3
  134.5 2.1 copy-start.4
  138.9 1.0 slice-start
  138.9 1.0 copy-start.8
  141.3 1.2 copy-start.2
  142.5 11.5 %copy-start.1 = (bf16[2,256,576]{1,2,0:T(8,128)(2,1)}, bf16[2,256,576]{1,2,0:T(8,128)(2,1)S(1)}, u32[]{:S(2)}) copy-start(bf16[2,256,576]{1,2,0:T(8,128)(2,1)S(1)} %get-tuple-element.672) | copy-start | bytes 1769476 | tf_op jit(solution)/shard_map/while
  143.9 2.0 copy-start.7
  148.7 1.1 copy-start.3
  148.7 2.1 copy-start.4
  154.4 1.0 slice-start
  154.4 1.0 copy-start.8
  156.8 1.2 copy-start.2
  158.0 11.5 %copy-start.1 = (bf16[2,256,576]{1,2,0:T(8,128)(2,1)}, bf16[2,256,576]{1,2,0:T(8,128)(2,1)S(1)}, u32[]{:S(2)}) copy-start(bf16[2,256,576]{1,2,0:T(8,128)(2,1)S(1)} %get-tuple-element.672) | copy-start | bytes 1769476 | tf_op jit(solution)/shard_map/while
  159.4 2.0 copy-start.7
  164.2 1.1 copy-start.3
  164.2 2.1 copy-start.4
  169.9 1.0 slice-start
  169.9 1.0 copy-start.8
  172.3 1.2 copy-start.2
  173.5 11.5 %copy-start.1 = (bf16[2,256,576]{1,2,0:T(8,128)(2,1)}, bf16[2,256,576]{1,2,0:T(8,128)(2,1)S(1)}, u32[]{:S(2)}) copy-start(bf16[2,256,576]{1,2,0:T(8,128)(2,1)S(1)} %get-tuple-element.672) | copy-start | bytes 1769476 | tf_op jit(solution)/shard_map/while
  174.9 2.0 copy-start.7
  179.7 1.1 copy-start.3
  179.8 2.1 copy-start.4
  185.4 1.0 slice-start
  185.5 1.0 copy-start.8
  187.8 1.2 copy-start.2
  189.0 8.0 %copy-start.15 = (bf16[64,576]{1,0:T(8,128)(2,1)S(1)}, bf16[64,576]{1,0:T(8,128)(2,1)}, u32[]{:S(2)}) copy-start(bf16[64,576]{1,0:T(8,128)(2,1)} %copy-done.14) | copy-start | bytes 221188
  189.0 8.0 %copy-start.18 = (bf16[64,256]{1,0:T(8,128)(2,1)S(1)}, bf16[64,256]{1,0:T(8,128)(2,1)}, u32[]{:S(2)}) copy-start(bf16[64,256]{1,0:T(8,128)(2,1)} %copy-done.17) | copy-start | bytes 98308
  189.0 212.5 %all-to-all-start = ((bf16[32,128,576]{1,2,0:T(8,128)(2,1)}), bf16[32,128,576]{1,2,0:T(8,128)(2,1)}, u32[]{:S(2)}, u32[]{:S(2)}) async-start(bf16[32,128,576]{1,2,0:T(8,128)(2,1)} %bitcast.265), calls=%async_computation | async-start | bytes 9437184 | tf_op jit(solution)/shard_map/all_to_all | solution.py:219
  197.0 320.8 %all-reduce.3.cloned.1.call-start = ((), (), s32[]{:S(2)}) async-start(), calls=%async_computation.2 | async-start | bytes 327680 | tf_op jit(solution)/shard_map/psum | solution.py:221
  404.6 114.1 %copy-start.12 = (bf16[128,576]{1,0:T(8,128)(2,1)S(1)}, bf16[128,576]{1,0:T(8,128)(2,1)}, u32[]{:S(2)}) copy-start(bf16[128,576]{1,0:T(8,128)(2,1)} %copy.37) | copy-start | bytes 442372
  404.6 114.1 %copy-start.21 = (f32[512]{0:T(512)S(1)}, f32[512]{0:T(512)}, u32[]{:S(2)}) copy-start(f32[512]{0:T(512)} %copy-done.20) | copy-start | bytes 6148
Sparse Core Ops, SparseCore 0:
  10.1 81.4 all-gather.1
  405.6 112.1 all-reduce.2
where the time goes:
time: 530 us; the launch traced here: 528 us
  waiting for transfers between devices  379 us (72%)
  local copies, waits for them, and re-layouts  54.2 us (10%)
  other arithmetic  38.9 us (7%)
  matrix products  31.8 us (6%)
  between operations  15.3 us (3%)
  starting transfers between devices  8 us (2%)
    all_to_all x1, waiting for transfers between devices, local(): lax.all_to_all(owner_terms, 'ctx', split_axis=0, concat_axis=0, tiled=True)  202 us
    psum x1, waiting for transfers between devices, local(): lax.psum(key_grads.astype(jnp.bfloat16), 'head').astype(jnp.float32)  110 us
    all_gather x1, waiting for transfers between devices, local(): gathered = lax.all_gather(kv_cache, 'ctx', axis=0, tiled=True)  66 us
    squeeze x16, local copies, waits for them, and re-layouts, local(): lax.map(lambda group_item: pair_scores(group_item[0], group_item[1]), (ke...  12.1 us
  transfers between devices with their start and end apart: 3, of which 3 were waited for; matrix products, arithmetic and copies ran while one was open for 4% of the time, Pallas kernels for 0%

commit v1 on v0

v1 whole, which is shorter than its diff:
```python
import functools

import jax
import jax.numpy as jnp
from jax import lax
from jax.experimental import pallas as pl
from jax.experimental.pallas import tpu as pltpu
from jax.sharding import PartitionSpec as P

MESH = pl.DeviceIdType.MESH
NEG_BIG = -1e30
EPS_NORM = 1e-06
LOG2_E = 1.4426950408889634

NZ = 16
HALF = NZ // 2
NP = 4
PIECE = 16
SPAN = 64
HEADS = 4
ROWS = SPAN * HEADS
LAT = 512
ROPE = 64
CAT = LAT + ROPE
NOPE = 128
CHUNK = 256
FIRST = 8
OTHER = 9
BLANK = 4 * OTHER

f32 = jnp.float32
bf16 = jnp.bfloat16


def dot(a, b, ca, cb):
    return lax.dot_general(a, b, (((ca,), (cb,)), ((), ())), preferred_element_type=f32)


def wrap(value, size):
    return lax.rem(value + 2 * size, size)


def kernel(
    q_nope, q_rope, kv, gain, w_uk, w_uv, attn_out, d_out, table,
    dq_nope_out, dq_rope_out, d_cache_out,
    keys, terms, sib_in, line_mid, line_in, ring_in, cross, final, result,
    queries, d_latent, delta, scores, d_prob, tops, other_terms, dq_prefix, dq_first,
    stats, sums, acc, inverse,
    sib0_s, sib0_r, gz_s, gz_r, gp_s, gp_r, gs_s, gs_r,
    ra_s, ra_r, rb_s, rb_r, rz_s, rz_r, rx_s, rx_r, rf_s, rf_r, rl_s, rl_r,
):
    scale = float(NOPE + ROPE) ** (-0.5)
    ctx = lax.axis_index("ctx")
    head = lax.axis_index("head")
    z, core = lax.div(ctx, 2), lax.rem(ctx, 2)
    x, y = lax.div(head, NP), lax.rem(head, NP)
    p = y * (1 - core) + x * core
    o = x * (1 - core) + y * core
    twin = 1 - core

    def at_own(pp):
        return {"ctx": ctx, "head": (1 - core) * (x * NP + pp) + core * (pp * NP + y)}

    def at_other(oo):
        return {"ctx": ctx, "head": (1 - core) * (oo * NP + y) + core * (x * NP + oo)}

    def at_z(zz):
        return {"ctx": zz * 2 + core, "head": head}

    sibling = {"ctx": z * 2 + twin, "head": head}
    right, left, far = wrap(p + 1, NP), wrap(p - 1, NP), wrap(p + 2, NP)
    up, down = wrap(z + 1, NZ), wrap(z - 1, NZ)

    def remote(src, dst, send, recv, device):
        return pltpu.make_async_remote_copy(
            src_ref=src, dst_ref=dst, send_sem=send, recv_sem=recv,
            device_id=device, device_id_type=MESH,
        )

    barrier = pltpu.get_barrier_semaphore()
    peers = [sibling, at_z(up), at_z(down)]
    peers += [at_own(wrap(p + j, NP)) for j in (1, 2, 3)]
    peers += [at_other(wrap(o + j, NP)) for j in (1, 2, 3)]
    for peer in peers:
        pl.semaphore_signal(barrier, inc=1, device_id=peer, device_id_type=MESH)

    raw = kv[:, :LAT].astype(f32)
    inv_norm = lax.rsqrt(jnp.mean(raw * raw, axis=-1, keepdims=True) + EPS_NORM)
    latent = (raw * inv_norm * gain[...].astype(f32)).astype(bf16)
    own_rope = kv[:, LAT:]
    for half in range(2):
        for pp in range(NP):
            rows = slice((half * NP + pp) * PIECE, (half * NP + pp + 1) * PIECE)
            keys[half, z, pp, core, :, :LAT] = latent[rows]
            keys[half, z, pp, core, :, LAT:] = own_rope[rows]

    pl.semaphore_wait(barrier, len(peers))
    first_copy = remote(
        keys.at[:, z, :, core], keys.at[:, z, :, core], sib0_s.at[0], sib0_r.at[0], sibling
    )
    first_copy.start()

    for h in range(HEADS):
        cols = slice(h * NOPE, (h + 1) * NOPE)
        rows = slice(h * SPAN, (h + 1) * SPAN)
        q_lat = dot(q_nope[:, cols], w_uk[h], 1, 0).astype(bf16)
        d_lat = dot(d_out[:, cols], w_uv[h], 1, 1).astype(bf16)
        for half in range(2):
            toks = slice(half * SPAN, (half + 1) * SPAN)
            queries[half, rows, :LAT] = q_lat[toks]
            queries[half, rows, LAT:] = q_rope[toks, h * ROPE : (h + 1) * ROPE]
            d_latent[half, rows, :] = d_lat[toks]
    for half in range(2):
        toks = slice(half * SPAN, (half + 1) * SPAN)
        prods = [
            d_out[toks, h * NOPE : (h + 1) * NOPE].astype(f32)
            * attn_out[toks, h * NOPE : (h + 1) * NOPE].astype(f32)
            for h in range(HEADS)
        ]
        prod = jnp.concatenate(prods, axis=0)
        delta[half] = jnp.sum(prod.T, axis=0, keepdims=True)

    def invert(b, carry):
        found = jnp.int32(0)
        for d in range(2 * NZ):
            found = found + jnp.where(table[d, 0] == b, d, 0)
        inverse[b] = jnp.minimum(found, 2 * NZ - 1)
        return carry

    lax.fori_loop(0, 2 * NZ, invert, 0)
    mine = table[ctx, 0]
    low_chunks = lax.div(mine + 4, 4)

    tops[...] = jnp.full(tops.shape, NEG_BIG, f32)
    dq_first[...] = jnp.zeros(dq_first.shape, f32)
    other_terms[BLANK] = jnp.zeros((SPAN, CAT), f32)

    first_copy.wait()

    def g_unit(ty, t):
        return wrap(z - t, NZ) if ty == 0 else wrap(z + t, NZ)

    g_last = (HALF, HALF - 1)

    def gz(ty, t):
        ref = keys.at[core, g_unit(ty, t), p]
        device = at_z(up) if ty == 0 else at_z(down)
        return remote(ref, ref, gz_s.at[ty, t], gz_r.at[ty, t], device)

    def gz_arrival(ty, t):
        ref = keys.at[core, g_unit(ty, t), p]
        device = at_z(up) if ty == 0 else at_z(down)
        return remote(ref, ref, gz_s.at[ty, t - 1], gz_r.at[ty, t - 1], device)

    def gp(ty, t, slot, piece, device):
        ref = keys.at[core, g_unit(ty, t), piece]
        return remote(ref, ref, gp_s.at[ty, t, slot], gp_r.at[ty, t, slot], device)

    def gs(ty, t, which):
        ref = keys.at[which, g_unit(ty, t)]
        return remote(ref, ref, gs_s.at[ty, t], gs_r.at[ty, t], sibling)

    def first_keys(t):
        low = keys[0, wrap(z - t, NZ)].reshape(CHUNK // 2, CAT)
        high = keys[0, wrap(z + lax.rem(t, HALF), NZ)].reshape(CHUNK // 2, CAT)
        return jnp.concatenate([low, high], axis=0)

    def fold_rows(value, op):
        part = value[0:8]
        for r in range(8, value.shape[0], 8):
            part = op(part, value[r : r + 8])
        return part

    def gather_step(t, carry):
        for ty in range(2):
            last = g_last[ty]

            @pl.when((t >= 1) & (t <= last))
            def _():
                gz_arrival(ty, t).wait_recv()

            @pl.when(t < last)
            def _():
                gz(ty, t).start()

            @pl.when((t >= 1) & (t <= last))
            def _():
                gp(ty, t, 0, p, at_own(right)).start()
                gp(ty, t, 1, p, at_own(left)).start()

        for ty in range(2):
            last = g_last[ty]

            @pl.when((t - 1 >= 1) & (t - 1 <= last))
            def _():
                tt = t - 1
                if ty == 0:
                    gp(ty, tt, 0, left, at_own(right)).wait_recv()
                    gp(ty, tt, 2, left, at_own(right)).start()
                    gp(ty, tt, 1, right, at_own(left)).wait_recv()
                else:
                    gp(ty, tt, 1, right, at_own(left)).wait_recv()
                    gp(ty, tt, 2, right, at_own(left)).start()
                    gp(ty, tt, 0, left, at_own(right)).wait_recv()

        for ty in range(2):
            last = g_last[ty]

            @pl.when((t - 2 >= 1) & (t - 2 <= last))
            def _():
                tt = t - 2
                gp(ty, tt, 2, far, at_own(right)).wait_recv()
                gs(ty, tt, core).start()

        for ty in range(2):
            last = g_last[ty]

            @pl.when((t - 3 >= 1) & (t - 3 <= last))
            def _():
                gs(ty, t - 3, twin).wait_recv()

        @pl.when(t - 3 >= 1)
        def _():
            tt = t - 3
            chunk = first_keys(tt)
            part = dot(chunk, queries[1], 1, 1)
            scores[tt - 1] = part
            tops[OTHER] = jnp.maximum(tops[OTHER], fold_rows(part, jnp.maximum))
            d_prob[tt - 1] = dot(chunk[:, :LAT], d_latent[1], 1, 1)

        return carry

    lax.fori_loop(0, HALF + 4, gather_step, 0)

    def kind_of(j):
        return jnp.where(j >= low_chunks, 1, 0)

    def other_keys(j):
        kind = kind_of(j)
        blocks = []
        for i in range(4):
            low_id = inverse[jnp.minimum(4 * j + i, 2 * NZ - 1)]
            high_id = inverse[jnp.clip(2 * NZ - 1 - (4 * (j - low_chunks) + i), 0, 2 * NZ - 1)]
            owner = jnp.where(kind == 1, high_id, low_id)
            block = keys[kind, lax.div(owner, 2), :, lax.rem(owner, 2)]
            blocks.append(block.reshape(SPAN, CAT))
        return jnp.concatenate(blocks, axis=0)

    key_in = lax.broadcasted_iota(jnp.int32, (CHUNK, ROWS), 0)
    tok_in = lax.rem(lax.broadcasted_iota(jnp.int32, (CHUNK, ROWS), 1), SPAN)

    def other_scores(j, carry):
        kind = kind_of(j)
        chunk = other_keys(j)
        low_gap = (4 * j - mine) * SPAN
        high_gap = (4 * (j - low_chunks) - (2 * NZ - 1 - mine)) * SPAN
        gap = jnp.where(kind == 1, high_gap, low_gap)
        part = dot(chunk, queries[kind], 1, 1)
        part = jnp.where(key_in + gap <= tok_in, part, NEG_BIG)
        scores[FIRST + j] = part
        tops[j] = fold_rows(part, jnp.maximum)
        d_prob[FIRST + j] = dot(chunk[:, :LAT], d_latent[kind], 1, 1)
        return carry

    lax.fori_loop(0, OTHER, other_scores, 0)

    top_low = jnp.full((8, ROWS), NEG_BIG, f32)
    top_high = tops[OTHER]
    for j in range(OTHER):
        high = j >= low_chunks
        top_low = jnp.maximum(top_low, jnp.where(high, NEG_BIG, tops[j]))
        top_high = jnp.maximum(top_high, jnp.where(high, tops[j], NEG_BIG))
    rate = scale * LOG2_E
    stats[0] = jnp.max(top_low, axis=0, keepdims=True) * rate
    stats[1] = jnp.max(top_high, axis=0, keepdims=True) * rate

    def exponents(n, carry):
        kind = jnp.where(n < FIRST, 1, kind_of(n - FIRST))
        part = jnp.exp2(scores[n] * rate - stats[kind])
        scores[n] = part
        sums[n] = fold_rows(part, jnp.add)
        return carry

    lax.fori_loop(0, FIRST + OTHER, exponents, 0)

    sum_low = jnp.zeros((8, ROWS), f32)
    sum_high = jnp.zeros((8, ROWS), f32)
    for n in range(FIRST):
        sum_high = sum_high + sums[n]
    for j in range(OTHER):
        high = j >= low_chunks
        sum_low = sum_low + jnp.where(high, 0.0, sums[FIRST + j])
        sum_high = sum_high + jnp.where(high, sums[FIRST + j], 0.0)
    stats[0] = 1.0 / jnp.sum(sum_low, axis=0, keepdims=True)
    stats[1] = 1.0 / jnp.sum(sum_high, axis=0, keepdims=True)

    def chunk_grads(n, kind, chunk):
        expo = scores[n]
        inv_sum = stats[kind]
        prob = (expo * inv_sum).astype(bf16)
        d_score = ((d_prob[n] - delta[kind]) * (expo * (inv_sum * scale))).astype(bf16)
        dq = dot(d_score, chunk, 0, 0)
        dk = dot(d_score, queries[kind], 1, 0)
        dk_lat = dk[:, :LAT] + dot(prob, d_latent[kind], 1, 0)
        return dq, dk_lat, dk[:, LAT:]

    def other_grads(j, carry):
        dq, dk_lat, dk_rope = chunk_grads(FIRST + j, kind_of(j), other_keys(j))
        for i in range(4):
            rows = slice(i * SPAN, (i + 1) * SPAN)
            other_terms[4 * j + i, :, :LAT] = dk_lat[rows]
            other_terms[4 * j + i, :, LAT:] = dk_rope[rows]

        fresh = (j == 0) | (j == low_chunks)
        before = dq_prefix[jnp.maximum(j - 1, 0)]
        dq_prefix[j] = dq + jnp.where(fresh, 0.0, before)
        return carry

    dq_prefix[0] = jnp.zeros((ROWS, CAT), f32)
    lax.fori_loop(0, OTHER, other_grads, 0)

    def r_unit(ty, k):
        return wrap(z + k, NZ) if ty == 0 else wrap(z - k, NZ)

    r_first = (HALF, HALF - 1)
    r_end = (0, 1)

    def ra(ty, k):
        unit = r_unit(ty, k)
        return remote(terms.at[twin, unit], sib_in.at[unit], ra_s.at[ty, k], ra_r.at[ty, k], sibling)

    def rb(ty, k, slot, piece, dst, device):
        unit = r_unit(ty, k)
        return remote(
            terms.at[core, unit, piece], dst, rb_s.at[ty, k, slot], rb_r.at[ty, k, slot], device
        )

    def rb_mid(ty, k):
        unit = r_unit(ty, k)
        device = at_own(right) if ty == 0 else at_own(left)
        return rb(ty, k, 0, far, line_mid.at[unit], device)

    def rb_right(ty, k):
        return rb(ty, k, 1, right, line_in.at[r_unit(ty, k), 0], at_own(right))

    def rb_left(ty, k):
        return rb(ty, k, 2, left, line_in.at[r_unit(ty, k), 1], at_own(left))

    def rz(ty, k):
        unit = r_unit(ty, k)
        device = at_z(up) if ty == 0 else at_z(down)
        return remote(
            terms.at[core, unit, p], ring_in.at[ty, unit], rz_s.at[ty, k], rz_r.at[ty, k], device
        )

    def rz_arrival(ty, k, unit):
        device = at_z(up) if ty == 0 else at_z(down)
        return remote(
            terms.at[core, unit, p], ring_in.at[ty, unit],
            rz_s.at[ty, k + 1], rz_r.at[ty, k + 1], device,
        )

    def valid(ty, k):
        return (k >= r_end[ty]) & (k <= r_first[ty])

    def first_grads(k):
        n = k - 1
        dq, dk_lat, dk_rope = chunk_grads(n, 1, first_keys(k))
        dq_first[...] += dq
        units = (wrap(z - k, NZ), wrap(z + lax.rem(k, HALF), NZ))
        for s in range(2):
            unit = units[s]
            for cc in range(2):
                block = table[unit * 2 + cc, 0]
                low_slot = jnp.where(block < 4 * low_chunks, block, BLANK)
                high_slot = jnp.minimum(4 * low_chunks + (2 * NZ - 1 - block), BLANK)
                low_term = other_terms[low_slot]
                high_term = other_terms[high_slot].astype(bf16)
                for pp in range(NP):
                    src = slice(s * 128 + (pp * 2 + cc) * PIECE, s * 128 + (pp * 2 + cc + 1) * PIECE)
                    rows = slice(pp * PIECE, (pp + 1) * PIECE)
                    terms[0, unit, pp, cc, :, :LAT] = (
                        dk_lat[src] + low_term[rows, :LAT]
                    ).astype(bf16)
                    terms[0, unit, pp, cc, :, LAT:] = (
                        dk_rope[src] + low_term[rows, LAT:]
                    ).astype(bf16)
                    terms[1, unit, pp, cc] = high_term[rows]

    def query_outputs():
        low = dq_prefix[low_chunks - 1]
        high = dq_prefix[OTHER - 1] + dq_first[...]
        for half, part in ((0, low), (1, high)):
            toks = slice(half * SPAN, (half + 1) * SPAN)
            dq_lat = part[:, :LAT].astype(bf16)
            dq_rope = part[:, LAT:]
            for h in range(HEADS):
                rows = slice(h * SPAN, (h + 1) * SPAN)
                dq_nope_out[toks, h * NOPE : (h + 1) * NOPE] = dot(
                    dq_lat[rows], w_uk[h], 1, 1
                ).astype(bf16)
            for h in range(0, HEADS, 2):
                pair = jnp.concatenate(
                    [
                        dq_rope[h * SPAN : (h + 1) * SPAN],
                        dq_rope[(h + 1) * SPAN : (h + 2) * SPAN],
                    ],
                    axis=1,
                )
                dq_rope_out[toks, h * ROPE : (h + 2) * ROPE] = pair.astype(bf16)

    def reduce_step(i, carry):
        @pl.when(i < HALF)
        def _():
            first_grads(HALF - i)

        k = HALF - i
        for ty in range(2):

            @pl.when(valid(ty, k))
            def _():
                ra(ty, k).start()

        for ty in range(2):
            ka = k + 1

            @pl.when(valid(ty, ka))
            def _():
                unit = r_unit(ty, ka)
                ra(ty, ka).wait_recv()
                both = terms[core, unit].astype(f32) + sib_in[unit].astype(f32)
                terms[core, unit] = both.astype(bf16)
                rb_mid(ty, ka).start()

        for ty in range(2):
            kb = k + 2

            @pl.when(valid(ty, kb))
            def _():
                unit = r_unit(ty, kb)
                rb_mid(ty, kb).wait_recv()
                piece = right if ty == 0 else left
                both = terms[core, unit, piece].astype(f32) + line_mid[unit].astype(f32)
                terms[core, unit, piece] = both.astype(bf16)
                rb_right(ty, kb).start()
                rb_left(ty, kb).start()

        for ty in range(2):
            kc = k + 3

            @pl.when(valid(ty, kc))
            def _():
                unit = r_unit(ty, kc)
                rb_right(ty, kc).wait_recv()
                rb_left(ty, kc).wait_recv()
                acc[...] = (
                    terms[core, unit, p].astype(f32)
                    + line_in[unit, 0].astype(f32)
                    + line_in[unit, 1].astype(f32)
                )

                @pl.when(kc < r_first[ty])
                def _():
                    rz_arrival(ty, kc, unit).wait_recv()
                    acc[...] += ring_in[ty, unit].astype(f32)

                if ty == 0:

                    @pl.when(kc == 0)
                    def _():
                        rz_arrival(1, 0, unit).wait_recv()
                        acc[...] += ring_in[1, unit].astype(f32)

                terms[core, unit, p] = acc[...].astype(bf16)

                @pl.when(kc >= 1)
                def _():
                    rz(ty, kc).start()

        @pl.when(i == HALF)
        def _():
            query_outputs()

        return carry

    lax.fori_loop(0, HALF + 4, reduce_step, 0)

    cross[o] = terms[core, z, p]

    def rx(j, slot):
        return remote(
            cross.at[slot], cross.at[slot], rx_s.at[j], rx_r.at[j], at_other(wrap(o + j, NP))
        )

    for j in (1, 2, 3):
        rx(j, o).start()
    for j in (1, 2, 3):
        rx(j, wrap(o - j, NP)).wait_recv()
    total = cross[0].astype(f32)
    for j in (1, 2, 3):
        total = total + cross[j].astype(f32)
    final[p] = total.astype(bf16)

    def rf(j, slot):
        return remote(
            final.at[slot], final.at[slot], rf_s.at[j], rf_r.at[j], at_own(wrap(p + j, NP))
        )

    for j in (1, 2, 3):
        rf(j, p).start()
    for j in (1, 2, 3):
        rf(j, wrap(p - j, NP)).wait_recv()

    def rl(which, half):
        return remote(final.at[:, which], result.at[half], rl_s.at[0], rl_r.at[0], sibling)

    rl(twin, core).start()
    result[core] = final[:, core]
    rl(core, twin).wait_recv()

    gain_row = gain[...].astype(f32)
    for half in range(2):
        toks = slice(half * SPAN, (half + 1) * SPAN)
        grads = result[half].reshape(SPAN, CAT).astype(f32)
        values = kv[toks, :LAT].astype(f32)
        inv = lax.rsqrt(jnp.mean(values * values, axis=-1, keepdims=True) + EPS_NORM)
        scaled = grads[:, :LAT] * gain_row
        inner = jnp.mean(values * scaled, axis=-1, keepdims=True)
        d_cache_out[toks, :LAT] = inv * scaled - values * (inv * inv * inv * inner)
        d_cache_out[toks, LAT:] = grads[:, LAT:]

    def gather_sends(t, carry):
        for ty in range(2):

            @pl.when(t < g_last[ty])
            def _():
                gz(ty, t).wait_send()

            @pl.when((t >= 1) & (t <= g_last[ty]))
            def _():
                gp(ty, t, 0, p, at_own(right)).wait_send()
                gp(ty, t, 1, p, at_own(left)).wait_send()
                if ty == 0:
                    gp(ty, t, 2, left, at_own(right)).wait_send()
                else:
                    gp(ty, t, 2, right, at_own(left)).wait_send()
                gs(ty, t, core).wait_send()

        return carry

    lax.fori_loop(0, HALF + 1, gather_sends, 0)

    def reduce_sends(k, carry):
        for ty in range(2):

            @pl.when(valid(ty, k))
            def _():
                ra(ty, k).wait_send()
                rb_mid(ty, k).wait_send()
                rb_right(ty, k).wait_send()
                rb_left(ty, k).wait_send()

                @pl.when(k >= 1)
                def _():
                    rz(ty, k).wait_send()

        return carry

    lax.fori_loop(0, HALF + 1, reduce_sends, 0)
    for j in (1, 2, 3):
        rx(j, o).wait_send()
        rf(j, p).wait_send()
    rl(twin, core).wait_send()


def local(q_nope, q_rope, kv_cache, kv_gain, w_uk, w_uv, attn_out, d_out, span_table):
    toks = q_nope.shape[0]
    vmem = pl.BlockSpec(memory_space=pltpu.VMEM)
    smem = pl.BlockSpec(memory_space=pltpu.SMEM)
    dma = pltpu.SemaphoreType.DMA
    scratch = [
        pltpu.VMEM((2, NZ, NP, 2, PIECE, CAT), bf16),
        pltpu.VMEM((2, NZ, NP, 2, PIECE, CAT), bf16),
        pltpu.VMEM((NZ, NP, 2, PIECE, CAT), bf16),
        pltpu.VMEM((NZ, 2, PIECE, CAT), bf16),
        pltpu.VMEM((NZ, 2, 2, PIECE, CAT), bf16),
        pltpu.VMEM((2, NZ, 2, PIECE, CAT), bf16),
        pltpu.VMEM((NP, 2, PIECE, CAT), bf16),
        pltpu.VMEM((NP, 2, PIECE, CAT), bf16),
        pltpu.VMEM((2, NP, PIECE, CAT), bf16),
        pltpu.VMEM((2, ROWS, CAT), bf16),
        pltpu.VMEM((2, ROWS, LAT), bf16),
        pltpu.VMEM((2, 1, ROWS), f32),
        pltpu.VMEM((FIRST + OTHER, CHUNK, ROWS), f32),
        pltpu.VMEM((FIRST + OTHER, CHUNK, ROWS), f32),
        pltpu.VMEM((OTHER + 1, 8, ROWS), f32),
        pltpu.VMEM((BLANK + 1, SPAN, CAT), f32),
        pltpu.VMEM((OTHER, ROWS, CAT), f32),
        pltpu.VMEM((ROWS, CAT), f32),
        pltpu.VMEM((2, 1, ROWS), f32),
        pltpu.VMEM((FIRST + OTHER, 8, ROWS), f32),
        pltpu.VMEM((2, PIECE, CAT), f32),
        pltpu.SMEM((2 * NZ,), jnp.int32),
        dma((1,)), dma((1,)),
        dma((2, HALF + 1)), dma((2, HALF + 1)),
        dma((2, HALF + 1, 3)), dma((2, HALF + 1, 3)),
        dma((2, HALF + 1)), dma((2, HALF + 1)),
        dma((2, HALF + 1)), dma((2, HALF + 1)),
        dma((2, HALF + 1, 3)), dma((2, HALF + 1, 3)),
        dma((2, HALF + 2)), dma((2, HALF + 2)),
        dma((NP,)), dma((NP,)),
        dma((NP,)), dma((NP,)),
        dma((1,)), dma((1,)),
    ]
    return pl.pallas_call(
        kernel,
        out_shape=(
            jax.ShapeDtypeStruct((toks, HEADS * NOPE), bf16),
            jax.ShapeDtypeStruct((toks, HEADS * ROPE), bf16),
            jax.ShapeDtypeStruct((toks, CAT), f32),
        ),
        in_specs=[vmem] * 8 + [smem],
        out_specs=(vmem, vmem, vmem),
        scratch_shapes=scratch,
        compiler_params=pltpu.CompilerParams(
            collective_id=0, has_side_effects=True, vmem_limit_bytes=56 * 1024 * 1024
        ),
    )(q_nope, q_rope, kv_cache, kv_gain.reshape(1, LAT), w_uk, w_uv, attn_out, d_out, span_table)


def solution(mesh):
    in_specs = (
        P("ctx", "head"),
        P("ctx", "head"),
        P("ctx", None),
        P(),
        P("head", None, None),
        P("head", None, None),
        P("ctx", "head"),
        P("ctx", "head"),
        P(),
    )
    out_specs = (P("ctx", "head"), P("ctx", "head"), P("ctx", None))
    return jax.shard_map(local, mesh=mesh, in_specs=in_specs, out_specs=out_specs, check_vma=False)
```

time: 530 us -> 116 us (0.22)
  waiting for transfers between devices: 379 us -> 0 us
  Pallas kernels: 0 us -> 108 us
  local copies, waits for them, and re-layouts: 54.2 us -> 7.04 us
  other arithmetic: 38.9 us -> 0 us
  matrix products: 31.8 us -> 0 us
  between operations: 15.3 us -> 0.66 us
  starting transfers between devices: 8 us -> 0 us
    all_to_all x1 -> x0, waiting for transfers between devices: 202 us -> none  [local(): lax.all_to_all(owner_terms, 'ctx', split_axis=0, concat_axis=0, tiled=True)]
    psum x1 -> x0, waiting for transfers between devices: 110 us -> none  [local(): lax.psum(key_grads.astype(jnp.bfloat16), 'head').astype(jnp.float32)]
    pallas_call x0 -> x1, Pallas kernels: none -> 108 us  [local(): pl.pallas_call(kernel, out_shape=(jax.ShapeDtypeStruct((toks, HEADS * NOP...]
    all_gather x1 -> x0, waiting for transfers between devices: 66 us -> none  [local(): gathered = lax.all_gather(kv_cache, 'ctx', axis=0, tiled=True)]
    dot_general x46 -> x0, matrix products: 31.2 us -> none  [the longest x4 5.83 us: pair_scores(): jnp.einsum('gkd,grd->gkr', other_keys, picked_query, preferred_element_ty...]
    squeeze x31 -> x0, local copies, waits for them, and re-layouts: 15.2 us -> none  [the longest x16 12.1 us: local(): lax.map(lambda group_item: pair_scores(group_item[0], group_item[1]), (ke...]
    reduce_sum x7 -> x0, other arithmetic: 9.7 us -> none  [the longest x2 3.37 us: latent_rows(): jnp.mean(values * values, axis=-1, keepdims=True) + eps_norm]
    add x12 -> x0, other arithmetic: 9.68 us -> none  [the longest x4 8.71 us: group_step(): return (dq_carry + dq_part, owner_terms)]
  transfers between devices with their start and end apart: 3 -> 0, of which waited for: 3 -> 0; matrix products, arithmetic and copies ran while one was open for 4% -> 0% of each run, Pallas kernels for 0% -> 0%
where the time goes in v1:
time: 116 us
  Pallas kernels  108 us (93%)
  local copies, waits for them, and re-layouts  7.04 us (6%)
    pallas_call x1, Pallas kernels, local(): pl.pallas_call(kernel, out_shape=(jax.ShapeDtypeStruct((toks, HEADS * NOP...  108 us
    unnamed x10, local copies, waits for them, and re-layouts  3.9 us

profile of v1, /device:TPU:1, one launch (start us, length us, event | category | flops | bytes accessed | tf_op | source)
XLA Modules:
  0.0 115.6 jit_solution(12622214253051044774)
XLA Ops:
  0.6 0.0 copy-start.2
  0.6 1.3 %reshape.9.gain = bf16[1,512]{1,0:T(2,128)(2,1)} reshape(bf16[512]{0:T(512)(128)(2,1)} %param.12) | data formatting | bytes 2048 | tf_op jit(solution)/shard_map/reshape | solution.py:628
  1.9 0.0 copy-done.2
  1.9 0.7 copy.13.table
  2.6 1.7 %copy.12.kv = bf16[128,576]{1,0:T(8,128)(2,1)} copy(bf16[128,576]{0,1:T(8,128)(2,1)} %param.11) | data formatting | bytes 294912 | tf_op args[2]
  4.3 107.9 %shard_map.112 = (bf16[128,512]{1,0:T(8,128)(2,1)}, bf16[128,256]{1,0:T(8,128)(2,1)}, f32[128,576]{1,0:T(8,128)}) custom-call(bf16[128,512]{1,0:T(8,128)(2,1)} %q_nope.1, bf16[128,256]{1,0:T(8,128)(2,1)} %q_rope.1, bf16[128,576]{1,0:T(8,128)(2,1)} %copy.12.kv, bf16[1,512]{1,0:T(2,128)(2,1)} %reshape.9.gain, bf16[4,128,512]{2,1,0:T(8,128)(2,1)} %w_uk.1, ...), custom_call_target="tpu_custom_call" | custom-call | tf_op jit(solution)/shard_map/pallas_call | solution.py:615
  112.2 0.0 copy-start
  112.2 1.9 %copy.14 = f32[128,576]{0,1:T(8,128)} copy(f32[128,576]{1,0:T(8,128)} %get-tuple-element.5) | data formatting | bytes 589824 | tf_op jit(solution)/shard_map/pallas_call | solution.py:615
  114.1 0.0 copy-done
  114.1 0.0 copy-start.1
  114.1 0.7 copy.17
  114.7 0.2 copy-done.1
  114.9 0.6 copy.18
Async XLA Ops:
  0.6 1.3 %copy-start.2 = (s32[32,2]{0,1:T(2,128)S(1)}, s32[32,2]{0,1:T(2,128)}, u32[]{:S(2)}) copy-start(s32[32,2]{0,1:T(2,128)} %param.17) | copy-start | bytes 772
  112.2 1.9 %copy-start = (bf16[128,512]{1,0:T(8,128)(2,1)S(1)}, bf16[128,512]{1,0:T(8,128)(2,1)}, u32[]{:S(2)}) copy-start(bf16[128,512]{1,0:T(8,128)(2,1)} %get-tuple-element.9) | copy-start | bytes 393220
  114.1 0.9 copy-start.1

commit v2 on v1

v2 whole, which is shorter than its diff:
```python
import functools

import jax
import jax.numpy as jnp
from jax import lax
from jax.experimental import pallas as pl
from jax.experimental.pallas import tpu as pltpu
from jax.sharding import PartitionSpec as P

MESH = pl.DeviceIdType.MESH
NEG_BIG = -1e30
EPS_NORM = 1e-06
LOG2_E = 1.4426950408889634

NZ = 16
HALF = NZ // 2
NP = 4
PIECE = 16
SPAN = 64
HEADS = 4
ROWS = SPAN * HEADS
LAT = 512
ROPE = 64
CAT = LAT + ROPE
NOPE = 128
CHUNK = 256
FIRST = 8
OTHER = 9
BLANK = 4 * OTHER

f32 = jnp.float32
bf16 = jnp.bfloat16


def dot(a, b, ca, cb):
    return lax.dot_general(a, b, (((ca,), (cb,)), ((), ())), preferred_element_type=f32)


def wrap(value, size):
    return lax.rem(value + 2 * size, size)


def kernel(
    q_nope_in, q_rope_in, kv_in, gain_in, w_uk_in, w_uv_in, attn_out_in, d_out_in, table,
    dq_nope_res, dq_rope_res, d_cache_res,
    q_nope, q_rope, kv_t, gain, w_uk, w_uv, attn_out, d_out,
    dq_nope_out, dq_rope_out, d_cache_out,
    keys, terms, sib_in, line_in, piece_in, ring_in, share, share_in, final, result,
    queries, d_latent, delta, scores, d_prob, tops, other_terms, dq_prefix, dq_first,
    stats, sums, inverse, in_sem, out_sem,
    g0_s, g0_r, gz_s, gz_r, gp_s, gp_r, gl_s, gl_r, gs_s, gs_r,
    ra_s, ra_r, rl_s, rl_r, rp_s, rp_r, rz_s, rz_r, rh_s, rh_r, f1_s, f1_r, f2_s, f2_r,
):
    scale = float(NOPE + ROPE) ** (-0.5)
    ctx = lax.axis_index("ctx")
    head = lax.axis_index("head")
    z, core = lax.div(ctx, 2), lax.rem(ctx, 2)
    x, y = lax.div(head, NP), lax.rem(head, NP)
    twin = 1 - core

    def at_x(j):
        return {"ctx": ctx, "head": wrap(x + j, NP) * NP + y}

    def at_y(j):
        return {"ctx": ctx, "head": x * NP + wrap(y + j, NP)}

    def at_z(zz):
        return {"ctx": zz * 2 + core, "head": head}

    sibling = {"ctx": z * 2 + twin, "head": head}

    def remote(src, dst, send, recv, device):
        return pltpu.make_async_remote_copy(
            src_ref=src, dst_ref=dst, send_sem=send, recv_sem=recv,
            device_id=device, device_id_type=MESH,
        )

    def by_core(step):
        for c in range(2):
            pl.when(core == c)(functools.partial(step, c))

    barrier = pltpu.get_barrier_semaphore()
    peers = [at_z(wrap(z + d, NZ)) for d in (8, 7, 9, 6, 10, 5, 11, 4, 12, 3, 13, 2, 14, 1, 15)]
    peers += [at_x(j) for j in (1, 2, 3)] + [at_y(j) for j in (1, 2, 3)] + [sibling]
    for peer in peers:
        pl.semaphore_signal(barrier, inc=1, device_id=peer, device_id_type=MESH)

    loads = [
        pltpu.make_async_copy(src, dst, in_sem.at[n])
        for n, (src, dst) in enumerate(
            (
                (kv_in, kv_t), (gain_in, gain), (q_nope_in, q_nope), (w_uk_in, w_uk),
                (q_rope_in, q_rope), (d_out_in, d_out), (w_uv_in, w_uv), (attn_out_in, attn_out),
            )
        )
    ]
    for load in loads:
        load.start()

    loads[0].wait()
    loads[1].wait()
    kv = kv_t[...].T
    raw = kv[:, :LAT].astype(f32)
    inv_norm = lax.rsqrt(jnp.mean(raw * raw, axis=-1, keepdims=True) + EPS_NORM)
    latent = (raw * inv_norm * gain[...].astype(f32)).astype(bf16)
    own_rope = kv[:, LAT:]
    for half in range(2):
        rows = slice(half * SPAN, (half + 1) * SPAN)
        keys[z, 2 * half + core, :, :, :LAT] = latent[rows].reshape(NP, PIECE, LAT)
        keys[z, 2 * half + core, :, :, LAT:] = own_rope[rows].reshape(NP, PIECE, ROPE)

    for load in loads[2:]:
        load.wait()
    for h in range(HEADS):
        cols = slice(h * NOPE, (h + 1) * NOPE)
        rows = slice(h * SPAN, (h + 1) * SPAN)
        q_lat = dot(q_nope[:, cols], w_uk[h], 1, 0).astype(bf16)
        d_lat = dot(d_out[:, cols], w_uv[h], 1, 1).astype(bf16)
        for half in range(2):
            toks = slice(half * SPAN, (half + 1) * SPAN)
            queries[half, rows, :LAT] = q_lat[toks]
            queries[half, rows, LAT:] = q_rope[toks, h * ROPE : (h + 1) * ROPE]
            d_latent[half, rows, :] = d_lat[toks]
    for half in range(2):
        toks = slice(half * SPAN, (half + 1) * SPAN)
        prods = [
            d_out[toks, h * NOPE : (h + 1) * NOPE].astype(f32)
            * attn_out[toks, h * NOPE : (h + 1) * NOPE].astype(f32)
            for h in range(HEADS)
        ]
        prod = jnp.concatenate(prods, axis=0)
        delta[half] = jnp.sum(prod.T, axis=0, keepdims=True)

    tops[...] = jnp.full(tops.shape, NEG_BIG, f32)
    dq_first[...] = jnp.zeros(dq_first.shape, f32)
    other_terms[BLANK] = jnp.zeros((SPAN, CAT), f32)

    pl.semaphore_wait(barrier, len(peers))

    def g_last(c):
        return HALF if c == 0 else HALF - 1

    def g_unit(c, d):
        return wrap(z - d, NZ) if c == 0 else wrap(z + d, NZ)

    def g_own(n):
        ref = keys.at[z, 2 * n + core]
        return remote(ref, ref, g0_s.at[n], g0_r.at[n], sibling)

    def g_own_arrival(n):
        ref = keys.at[z, 2 * n + twin]
        return remote(ref, ref, g0_s.at[n], g0_r.at[n], sibling)

    def gz(c, d, unit):
        ref = keys.at[unit, x, y]
        device = at_z(wrap(z + d, NZ) if c == 0 else wrap(z - d, NZ))
        return remote(ref, ref, gz_s.at[d], gz_r.at[d], device)

    def gp(c, d, j, back):
        unit = g_unit(c, d)
        if c == 0:
            ref, device = keys.at[unit, wrap(x - back, NP), y], at_x(j)
        else:
            ref, device = keys.at[unit, x, wrap(y - back, NP)], at_y(j)
        return remote(ref, ref, gp_s.at[d, j], gp_r.at[d, j], device)

    def gl(c, d, j, back):
        unit = g_unit(c, d)
        if c == 0:
            ref, device = keys.at[unit, :, wrap(y - back, NP)], at_y(j)
        else:
            ref, device = keys.at[unit, wrap(x - back, NP)], at_x(j)
        return remote(ref, ref, gl_s.at[d, j], gl_r.at[d, j], device)

    def gs(c, d):
        ref = keys.at[g_unit(c, d)]
        return remote(ref, ref, gs_s.at[d], gs_r.at[d], sibling)

    for n in range(2):
        g_own(n).start()
    for n in range(2):
        g_own_arrival(n).wait_recv()

    def each(low, high, step):
        def body(d, carry):
            step(d)
            return carry

        lax.fori_loop(low, high, body, 0)

    def spread_z(c):
        each(1, g_last(c) + 1, lambda d: gz(c, d, z).start())

    by_core(spread_z)

    def invert(b, carry):
        found = jnp.int32(0)
        for d in range(2 * NZ):
            found = found + jnp.where(table[0, d] == b, d, 0)
        inverse[b] = jnp.minimum(found, 2 * NZ - 1)
        return carry

    lax.fori_loop(0, 2 * NZ, invert, 0)
    mine = table[0, ctx]
    low_chunks = lax.div(mine + 4, 4)

    def spread_piece(c):
        def step(d):
            gz(c, d, g_unit(c, d)).wait_recv()
            for j in (2, 1, 3):
                gp(c, d, j, 0).start()

        each(1, g_last(c) + 1, step)

    by_core(spread_piece)

    def spread_line(c):
        def step(d):
            for j in (1, 2, 3):
                gp(c, d, j, j).wait_recv()
            for j in (2, 1, 3):
                gl(c, d, j, 0).start()

        each(1, g_last(c) + 1, step)

    by_core(spread_line)

    def first_keys(t):
        low = keys[wrap(z - t, NZ), 0:2].reshape(CHUNK // 2, CAT)
        high = keys[wrap(z + lax.rem(t, HALF), NZ), 0:2].reshape(CHUNK // 2, CAT)
        return jnp.concatenate([low, high], axis=0)

    def fold_rows(value, op):
        part = value[0:8]
        for r in range(8, value.shape[0], 8):
            part = op(part, value[r : r + 8])
        return part

    def arrivals(d):
        def own(c):
            @pl.when(d <= g_last(c))
            def _():
                for j in (1, 2, 3):
                    gl(c, d, j, j).wait_recv()
                gs(c, d).start()

            @pl.when((d >= 2) & (d - 1 <= g_last(1 - c)))
            def _():
                gs(1 - c, d - 1).wait_recv()

        by_core(own)

        @pl.when(d >= 2)
        def _():
            t = d - 1
            chunk = first_keys(t)
            part = dot(chunk, queries[1], 1, 1)
            scores[t - 1] = part
            tops[OTHER] = jnp.maximum(tops[OTHER], fold_rows(part, jnp.maximum))
            d_prob[t - 1] = dot(chunk[:, :LAT], d_latent[1], 1, 1)

    each(1, HALF + 2, arrivals)

    def kind_of(j):
        return jnp.where(j >= low_chunks, 1, 0)

    def other_keys(j):
        kind = kind_of(j)
        blocks = []
        for i in range(4):
            low_id = inverse[jnp.minimum(4 * j + i, 2 * NZ - 1)]
            high_id = inverse[jnp.clip(2 * NZ - 1 - (4 * (j - low_chunks) + i), 0, 2 * NZ - 1)]
            owner = jnp.where(kind == 1, high_id, low_id)
            block = keys[lax.div(owner, 2), 2 * kind + lax.rem(owner, 2)]
            blocks.append(block.reshape(SPAN, CAT))
        return jnp.concatenate(blocks, axis=0)

    key_in = lax.broadcasted_iota(jnp.int32, (CHUNK, ROWS), 0)
    tok_in = lax.rem(lax.broadcasted_iota(jnp.int32, (CHUNK, ROWS), 1), SPAN)

    def other_scores(j, carry):
        kind = kind_of(j)
        chunk = other_keys(j)
        low_gap = (4 * j - mine) * SPAN
        high_gap = (4 * (j - low_chunks) - (2 * NZ - 1 - mine)) * SPAN
        gap = jnp.where(kind == 1, high_gap, low_gap)
        part = dot(chunk, queries[kind], 1, 1)
        part = jnp.where(key_in + gap <= tok_in, part, NEG_BIG)
        scores[FIRST + j] = part
        tops[j] = fold_rows(part, jnp.maximum)
        d_prob[FIRST + j] = dot(chunk[:, :LAT], d_latent[kind], 1, 1)
        return carry

    lax.fori_loop(0, OTHER, other_scores, 0)

    top_low = jnp.full((8, ROWS), NEG_BIG, f32)
    top_high = tops[OTHER]
    for j in range(OTHER):
        high = j >= low_chunks
        top_low = jnp.maximum(top_low, jnp.where(high, NEG_BIG, tops[j]))
        top_high = jnp.maximum(top_high, jnp.where(high, tops[j], NEG_BIG))
    rate = scale * LOG2_E
    stats[0] = jnp.max(top_low, axis=0, keepdims=True) * rate
    stats[1] = jnp.max(top_high, axis=0, keepdims=True) * rate

    def exponents(n, carry):
        kind = jnp.where(n < FIRST, 1, kind_of(n - FIRST))
        part = jnp.exp2(scores[n] * rate - stats[kind])
        scores[n] = part
        sums[n] = fold_rows(part, jnp.add)
        return carry

    lax.fori_loop(0, FIRST + OTHER, exponents, 0)

    sum_low = jnp.zeros((8, ROWS), f32)
    sum_high = jnp.zeros((8, ROWS), f32)
    for n in range(FIRST):
        sum_high = sum_high + sums[n]
    for j in range(OTHER):
        high = j >= low_chunks
        sum_low = sum_low + jnp.where(high, 0.0, sums[FIRST + j])
        sum_high = sum_high + jnp.where(high, sums[FIRST + j], 0.0)
    stats[0] = 1.0 / jnp.sum(sum_low, axis=0, keepdims=True)
    stats[1] = 1.0 / jnp.sum(sum_high, axis=0, keepdims=True)

    def chunk_grads(n, kind, chunk):
        expo = scores[n]
        inv_sum = stats[kind]
        prob = (expo * inv_sum).astype(bf16)
        d_score = ((d_prob[n] - delta[kind]) * (expo * (inv_sum * scale))).astype(bf16)
        dq = dot(d_score, chunk, 0, 0)
        dk = dot(d_score, queries[kind], 1, 0)
        dk_lat = dk[:, :LAT] + dot(prob, d_latent[kind], 1, 0)
        return dq, dk_lat, dk[:, LAT:]

    def other_grads(j, carry):
        dq, dk_lat, dk_rope = chunk_grads(FIRST + j, kind_of(j), other_keys(j))
        for i in range(4):
            rows = slice(i * SPAN, (i + 1) * SPAN)
            other_terms[4 * j + i, :, :LAT] = dk_lat[rows]
            other_terms[4 * j + i, :, LAT:] = dk_rope[rows]

        fresh = (j == 0) | (j == low_chunks)
        before = dq_prefix[jnp.maximum(j - 1, 0)]
        dq_prefix[j] = dq + jnp.where(fresh, 0.0, before)
        return carry

    dq_prefix[0] = jnp.zeros((ROWS, CAT), f32)
    lax.fori_loop(0, OTHER, other_grads, 0)

    def r_first(c):
        return HALF if c == 0 else HALF - 1

    def r_end(c):
        return 1 if c == 0 else 0

    def r_unit(c, k):
        return wrap(z + k, NZ) if c == 0 else wrap(z - k, NZ)

    def ra(c, k):
        return remote(terms.at[r_unit(c, k)], sib_in.at[k], ra_s.at[k], ra_r.at[k], sibling)

    def rl(c, k, j):
        unit = r_unit(c, k)
        if c == 0:
            ref, device = terms.at[unit, :, wrap(y + j, NP)], at_y(j)
        else:
            ref, device = terms.at[unit, wrap(x + j, NP)], at_x(j)
        return remote(ref, line_in.at[k, j - 1], rl_s.at[k, j], rl_r.at[k, j], device)

    def rp(c, k, j):
        unit = r_unit(c, k)
        if c == 0:
            ref, device = terms.at[unit, wrap(x + j, NP), y], at_x(j)
        else:
            ref, device = terms.at[unit, x, wrap(y + j, NP)], at_y(j)
        return remote(ref, piece_in.at[k, j - 1], rp_s.at[k, j], rp_r.at[k, j], device)

    def rz(c, k):
        unit = r_unit(c, k)
        return remote(terms.at[unit, x, y], ring_in.at[k], rz_s.at[k], rz_r.at[k], at_z(unit))

    def first_grads(k):
        n = k - 1
        dq, dk_lat, dk_rope = chunk_grads(n, 1, first_keys(k))
        dq_first[...] += dq
        units = (wrap(z - k, NZ), wrap(z + lax.rem(k, HALF), NZ))
        for s in range(2):
            unit = units[s]
            for cc in range(2):
                block = table[0, unit * 2 + cc]
                low_slot = jnp.where(block < 4 * low_chunks, block, BLANK)
                high_slot = jnp.minimum(4 * low_chunks + (2 * NZ - 1 - block), BLANK)
                low_term = other_terms[low_slot]
                rows = slice((2 * s + cc) * SPAN, (2 * s + cc + 1) * SPAN)
                terms[unit, cc, :, :, :LAT] = (
                    (dk_lat[rows] + low_term[:, :LAT]).astype(bf16).reshape(NP, PIECE, LAT)
                )
                terms[unit, cc, :, :, LAT:] = (
                    (dk_rope[rows] + low_term[:, LAT:]).astype(bf16).reshape(NP, PIECE, ROPE)
                )
                terms[unit, 2 + cc] = other_terms[high_slot].astype(bf16).reshape(NP, PIECE, CAT)

    def reduce_step(i):
        @pl.when(i < HALF)
        def _():
            first_grads(HALF - i)

        k = HALF - i

        def own(c):
            @pl.when((k >= r_end(1 - c)) & (k <= r_first(1 - c)))
            def _():
                ra(1 - c, k).start()

            ka = k + 1

            @pl.when((ka >= r_end(c)) & (ka <= r_first(c)))
            def _():
                unit = r_unit(c, ka)
                ra(c, ka).wait_recv()
                both = terms[unit].astype(f32) + sib_in[ka].astype(f32)
                terms[unit] = both.astype(bf16)
                for j in (2, 1, 3):
                    rl(c, ka, j).start()

        by_core(own)

    each(0, HALF + 2, reduce_step)

    low = dq_prefix[low_chunks - 1]
    high = dq_prefix[OTHER - 1] + dq_first[...]
    for half, part in ((0, low), (1, high)):
        toks = slice(half * SPAN, (half + 1) * SPAN)
        dq_lat = part[:, :LAT].astype(bf16)
        dq_rope = part[:, LAT:]
        for h in range(HEADS):
            rows = slice(h * SPAN, (h + 1) * SPAN)
            dq_nope_out[toks, h * NOPE : (h + 1) * NOPE] = dot(
                dq_lat[rows], w_uk[h], 1, 1
            ).astype(bf16)
        for h in range(0, HEADS, 2):
            pair = jnp.concatenate(
                [dq_rope[h * SPAN : (h + 1) * SPAN], dq_rope[(h + 1) * SPAN : (h + 2) * SPAN]],
                axis=1,
            )
            dq_rope_out[toks, h * ROPE : (h + 2) * ROPE] = pair.astype(bf16)
    stores = [
        pltpu.make_async_copy(dq_nope_out, dq_nope_res, out_sem.at[0]),
        pltpu.make_async_copy(dq_rope_out, dq_rope_res, out_sem.at[1]),
    ]
    for store in stores:
        store.start()

    def sum_lines(c):
        def step(i):
            k = HALF - i

            @pl.when((k >= r_end(c)) & (k <= r_first(c)))
            def _():
                unit = r_unit(c, k)
                for j in (1, 2, 3):
                    rl(c, k, j).wait_recv()
                total = terms[unit, :, y] if c == 0 else terms[unit, x]
                total = total.astype(f32)
                for j in range(3):
                    total = total + line_in[k, j].astype(f32)
                if c == 0:
                    terms[unit, :, y] = total.astype(bf16)
                else:
                    terms[unit, x] = total.astype(bf16)
                for j in (2, 1, 3):
                    rp(c, k, j).start()

        each(0, HALF + 1, step)

    by_core(sum_lines)

    def sum_pieces(c):
        def step(i):
            k = HALF - i

            @pl.when((k >= r_end(c)) & (k <= r_first(c)))
            def _():
                unit = r_unit(c, k)
                for j in (1, 2, 3):
                    rp(c, k, j).wait_recv()
                total = terms[unit, x, y].astype(f32)
                for j in range(3):
                    total = total + piece_in[k, j].astype(f32)
                terms[unit, x, y] = total.astype(bf16)

                @pl.when(k >= 1)
                def _():
                    rz(c, k).start()

        each(0, HALF + 1, step)

    by_core(sum_pieces)

    def sum_ring(c):
        share[...] = jnp.zeros((PIECE, CAT), f32) if c == 0 else terms[z, x, y].astype(f32)

        def step(k):
            rz(c, k).wait_recv()
            share[...] += ring_in[k].astype(f32)

        each(1, r_first(c) + 1, step)

    by_core(sum_ring)

    holds = lax.rem(x, 2) == core
    half_of = lax.div(x, 2)

    def rh():
        return remote(share, share_in, rh_s.at[0], rh_r.at[0], sibling)

    def f1(j, back):
        ref = final.at[wrap(y - back, NP)]
        return remote(ref, ref, f1_s.at[j], f1_r.at[j], at_y(j))

    def f2(j, back):
        ref = result.at[lax.div(wrap(x - back, NP), 2)]
        return remote(final, ref, f2_s.at[j], f2_r.at[j], at_x(j))

    @pl.when(holds)
    def _():
        rh().wait_recv()
        final[y] = (share[...] + share_in[...]).astype(bf16)
        for j in (2, 1, 3):
            f1(j, 0).start()
        for j in (1, 2, 3):
            f1(j, j).wait_recv()
        for j in (2, 1, 3):
            f2(j, 0).start()
        result[half_of] = final[...]

    @pl.when(jnp.logical_not(holds))
    def _():
        rh().start()

    for j in (1, 2, 3):

        @pl.when(lax.rem(x + NP - j, 2) == core)
        def _():
            f2(j, j).wait_recv()

    gain_row = gain[...].astype(f32)
    kv_rows = kv_t[...].T
    grads = result[...].reshape(2 * SPAN, CAT).astype(f32)
    values = kv_rows[:, :LAT].astype(f32)
    inv = lax.rsqrt(jnp.mean(values * values, axis=-1, keepdims=True) + EPS_NORM)
    scaled = grads[:, :LAT] * gain_row
    inner = jnp.mean(values * scaled, axis=-1, keepdims=True)
    d_raw = inv * scaled - values * (inv * inv * inv * inner)
    d_cache_out[:LAT, :] = d_raw.T
    d_cache_out[LAT:, :] = grads[:, LAT:].T
    store = pltpu.make_async_copy(d_cache_out, d_cache_res, out_sem.at[2])
    store.start()

    for n in range(2):
        g_own(n).wait_send()

    def sends(c):
        def gather_step(d):
            gz(c, d, z).wait_send()
            for j in (1, 2, 3):
                gp(c, d, j, 0).wait_send()
                gl(c, d, j, 0).wait_send()
            gs(c, d).wait_send()

        each(1, g_last(c) + 1, gather_step)

        def reduce_twin(k):
            ra(1 - c, k).wait_send()

        each(r_end(1 - c), r_first(1 - c) + 1, reduce_twin)

        def reduce_step(k):
            for j in (1, 2, 3):
                rl(c, k, j).wait_send()
                rp(c, k, j).wait_send()

        each(r_end(c), r_first(c) + 1, reduce_step)
        each(1, r_first(c) + 1, lambda k: rz(c, k).wait_send())

    by_core(sends)

    @pl.when(holds)
    def _():
        for j in (1, 2, 3):
            f1(j, 0).wait_send()
            f2(j, 0).wait_send()

    @pl.when(jnp.logical_not(holds))
    def _():
        rh().wait_send()

    for done in stores:
        done.wait()
    store.wait()


def local(q_nope, q_rope, kv_cache, kv_gain, w_uk, w_uv, attn_out, d_out, span_table):
    toks = q_nope.shape[0]
    hbm = pl.BlockSpec(memory_space=pl.ANY)
    smem = pl.BlockSpec(memory_space=pltpu.SMEM)
    dma = pltpu.SemaphoreType.DMA
    inputs = (
        q_nope, q_rope, kv_cache.T, kv_gain.reshape(1, LAT), w_uk, w_uv, attn_out, d_out
    )
    out_shape = (
        jax.ShapeDtypeStruct((toks, HEADS * NOPE), bf16),
        jax.ShapeDtypeStruct((toks, HEADS * ROPE), bf16),
        jax.ShapeDtypeStruct((CAT, toks), f32),
    )
    scratch = [pltpu.VMEM(value.shape, value.dtype) for value in inputs]
    scratch += [pltpu.VMEM(value.shape, value.dtype) for value in out_shape]
    scratch += [
        pltpu.VMEM((NZ, NP, NP, PIECE, CAT), bf16),
        pltpu.VMEM((NZ, NP, NP, PIECE, CAT), bf16),
        pltpu.VMEM((HALF + 1, NP, NP, PIECE, CAT), bf16),
        pltpu.VMEM((HALF + 1, 3, NP, PIECE, CAT), bf16),
        pltpu.VMEM((HALF + 1, 3, PIECE, CAT), bf16),
        pltpu.VMEM((HALF + 1, PIECE, CAT), bf16),
        pltpu.VMEM((PIECE, CAT), f32),
        pltpu.VMEM((PIECE, CAT), f32),
        pltpu.VMEM((NP, PIECE, CAT), bf16),
        pltpu.VMEM((2, NP, PIECE, CAT), bf16),
        pltpu.VMEM((2, ROWS, CAT), bf16),
        pltpu.VMEM((2, ROWS, LAT), bf16),
        pltpu.VMEM((2, 1, ROWS), f32),
        pltpu.VMEM((FIRST + OTHER, CHUNK, ROWS), f32),
        pltpu.VMEM((FIRST + OTHER, CHUNK, ROWS), f32),
        pltpu.VMEM((OTHER + 1, 8, ROWS), f32),
        pltpu.VMEM((BLANK + 1, SPAN, CAT), f32),
        pltpu.VMEM((OTHER, ROWS, CAT), f32),
        pltpu.VMEM((ROWS, CAT), f32),
        pltpu.VMEM((2, 1, ROWS), f32),
        pltpu.VMEM((FIRST + OTHER, 8, ROWS), f32),
        pltpu.SMEM((2 * NZ,), jnp.int32),
        dma((len(inputs),)),
        dma((3,)),
        dma((2,)), dma((2,)),
        dma((HALF + 1,)), dma((HALF + 1,)),
        dma((HALF + 1, NP)), dma((HALF + 1, NP)),
        dma((HALF + 1, NP)), dma((HALF + 1, NP)),
        dma((HALF + 1,)), dma((HALF + 1,)),
        dma((HALF + 1,)), dma((HALF + 1,)),
        dma((HALF + 1, NP)), dma((HALF + 1, NP)),
        dma((HALF + 1, NP)), dma((HALF + 1, NP)),
        dma((HALF + 1,)), dma((HALF + 1,)),
        dma((1,)), dma((1,)),
        dma((NP,)), dma((NP,)),
        dma((NP,)), dma((NP,)),
    ]
    d_q_nope, d_q_rope, d_cache = pl.pallas_call(
        kernel,
        out_shape=out_shape,
        in_specs=[hbm] * len(inputs) + [smem],
        out_specs=(hbm, hbm, hbm),
        scratch_shapes=scratch,
        compiler_params=pltpu.CompilerParams(
            collective_id=0, has_side_effects=True, vmem_limit_bytes=60 * 1024 * 1024
        ),
    )(*inputs, span_table.T)
    return d_q_nope, d_q_rope, d_cache.T


def solution(mesh):
    in_specs = (
        P("ctx", "head"),
        P("ctx", "head"),
        P("ctx", None),
        P(),
        P("head", None, None),
        P("head", None, None),
        P("ctx", "head"),
        P("ctx", "head"),
        P(),
    )
    out_specs = (P("ctx", "head"), P("ctx", "head"), P("ctx", None))
    return jax.shard_map(local, mesh=mesh, in_specs=in_specs, out_specs=out_specs, check_vma=False)
```

time: 116 us -> 108 us (0.931)
  Pallas kernels: 108 us -> 102 us
  local copies, waits for them, and re-layouts: 7.04 us -> 5.05 us
    pallas_call x1, Pallas kernels: 108 us -> 102 us  [local(): pl.pallas_call(kernel, out_shape=out_shape, in_specs=[hbm] * len(inputs)...]
    pallas_call x1 -> x0, local copies, waits for them, and re-layouts: 1.87 us -> none  [local(): pl.pallas_call(kernel, out_shape=(jax.ShapeDtypeStruct((toks, HEADS * NOP...]
    unnamed x10 -> x7, local copies, waits for them, and re-layouts: 3.9 us -> 4.47 us
where the time goes in v2:
time: 108 us
  Pallas kernels  102 us (94%)
  local copies, waits for them, and re-layouts  5.05 us (5%)
    pallas_call x1, Pallas kernels, local(): pl.pallas_call(kernel, out_shape=out_shape, in_specs=[hbm] * len(inputs)...  102 us
    unnamed x7, local copies, waits for them, and re-layouts  4.47 us

profile of v2, /device:TPU:1, one launch (start us, length us, event | category | flops | bytes accessed | tf_op | source)
XLA Modules:
  0.0 107.7 jit_solution(7728262354994211776)
XLA Ops:
  0.6 0.0 copy-start.1
  0.6 0.7 copy-done.1
  1.3 0.6 reshape.9.gain_in
  1.9 102.0 %shard_map.112 = (bf16[128,512]{1,0:T(8,128)(2,1)}, bf16[128,256]{1,0:T(8,128)(2,1)}, f32[576,128]{1,0:T(8,128)}) custom-call(bf16[128,512]{1,0:T(8,128)(2,1)} %q_nope_in.1, bf16[128,256]{1,0:T(8,128)(2,1)} %q_rope_in.1, bf16[576,128]{1,0:T(8,128)(2,1)} %bitcast.4, bf16[1,512]{1,0:T(2,128)(2,1)} %reshape.9.gain_in, bf16[4,128,512]{2,1,0:T(8,128)(2,1)} %w_uk_in.1, ...), custom_call_target="tpu_custom_call" | custom-call | tf_op jit(solution)/shard_map/pallas_call | solution.py:657
  103.9 0.0 copy-start
  103.9 1.6 %copy.15 = bf16[128,512]{1,0:T(8,128)(2,1)} copy(bf16[128,512]{1,0:T(8,128)(2,1)} %get-tuple-element.12) | data formatting | bytes 262144
  105.5 1.5 %copy.16 = bf16[128,256]{1,0:T(8,128)(2,1)} copy(bf16[128,256]{1,0:T(8,128)(2,1)} %get-tuple-element.13) | data formatting | bytes 131072
  107.0 0.0 copy-done
  107.0 0.7 copy.17
Async XLA Ops:
  0.6 0.7 copy-start.1
  103.9 3.1 %copy-start = (f32[576,128]{1,0:T(8,128)S(1)}, f32[576,128]{1,0:T(8,128)}, u32[]{:S(2)}) copy-start(f32[576,128]{1,0:T(8,128)} %get-tuple-element.8) | copy-start | bytes 884740

commit v3 on v2

--- a/solution.py
+++ b/solution.py
@@ -21,6 +21,8 @@
 ROWS = SPAN * HEADS
 LAT = 512
 ROPE = 64
+LAG_G = 4
+LAG_R = 2
 CAT = LAT + ROPE
 NOPE = 128
 CHUNK = 256
@@ -45,11 +47,11 @@
     dq_nope_res, dq_rope_res, d_cache_res,
     q_nope, q_rope, kv_t, gain, w_uk, w_uv, attn_out, d_out,
     dq_nope_out, dq_rope_out, d_cache_out,
-    keys, terms, sib_in, line_in, piece_in, ring_in, share, share_in, final, result,
+    keys, terms, sib_in, line_in, piece_in, ring_in, share, result,
     queries, d_latent, delta, scores, d_prob, tops, other_terms, dq_prefix, dq_first,
     stats, sums, inverse, in_sem, out_sem,
     g0_s, g0_r, gz_s, gz_r, gp_s, gp_r, gl_s, gl_r, gs_s, gs_r,
-    ra_s, ra_r, rl_s, rl_r, rp_s, rp_r, rz_s, rz_r, rh_s, rh_r, f1_s, f1_r, f2_s, f2_r,
+    ra_s, ra_r, rl_s, rl_r, rp_s, rp_r, rz_s, rz_r, f1_s, f1_r,
 ):
     scale = float(NOPE + ROPE) ** (-0.5)
     ctx = lax.axis_index("ctx")
@@ -79,11 +81,38 @@
         for c in range(2):
             pl.when(core == c)(functools.partial(step, c))
 
+    holds = lax.rem(x, 2) == core
+    holder = lax.rem(x, 2)
+
+    def at_plane(i, j):
+        return {"ctx": ctx, "head": wrap(x + i, NP) * NP + wrap(y + j, NP)}
+
     barrier = pltpu.get_barrier_semaphore()
-    peers = [at_z(wrap(z + d, NZ)) for d in (8, 7, 9, 6, 10, 5, 11, 4, 12, 3, 13, 2, 14, 1, 15)]
-    peers += [at_x(j) for j in (1, 2, 3)] + [at_y(j) for j in (1, 2, 3)] + [sibling]
-    for peer in peers:
-        pl.semaphore_signal(barrier, inc=1, device_id=peer, device_id_type=MESH)
+
+    def signal(device):
+        pl.semaphore_signal(barrier, inc=1, device_id=device, device_id_type=MESH)
+
+    def greet(c):
+        for d in range(HALF if c == 0 else HALF - 1, 0, -1):
+            signal({"ctx": wrap(z - d if c == 0 else z + d, NZ) * 2 + c, "head": head})
+
+        @pl.when(holds)
+        def _():
+            for d in range(HALF - 1 if c == 0 else HALF, 0, -1):
+                signal({"ctx": wrap(z + d if c == 0 else z - d, NZ) * 2 + 1 - c, "head": head})
+
+    by_core(greet)
+    for i in range(NP):
+        for j in range(NP):
+            if i and j:
+
+                @pl.when(lax.rem(x + i, 2) == core)
+                def _():
+                    signal(at_plane(i, j))
+
+            elif i or j:
+                signal(at_plane(i, j))
+    signal(sibling)
 
     loads = [
         pltpu.make_async_copy(src, dst, in_sem.at[n])
@@ -102,7 +131,7 @@
     kv = kv_t[...].T
     raw = kv[:, :LAT].astype(f32)
     inv_norm = lax.rsqrt(jnp.mean(raw * raw, axis=-1, keepdims=True) + EPS_NORM)
-    latent = (raw * inv_norm * gain[...].astype(f32)).astype(bf16)
+    latent = (raw * inv_norm * gain[...].reshape(1, LAT).astype(f32)).astype(bf16)
     own_rope = kv[:, LAT:]
     for half in range(2):
         rows = slice(half * SPAN, (half + 1) * SPAN)
@@ -135,7 +164,9 @@
     dq_first[...] = jnp.zeros(dq_first.shape, f32)
     other_terms[BLANK] = jnp.zeros((SPAN, CAT), f32)
 
-    pl.semaphore_wait(barrier, len(peers))
+    z_targets = HALF - core
+    targets = 2 * (NP - 1) + 1 + z_targets
+    pl.semaphore_wait(barrier, jnp.where(holds, targets + (NP - 1) ** 2, targets + z_targets))
 
     def g_last(c):
         return HALF if c == 0 else HALF - 1
@@ -204,26 +235,26 @@
     mine = table[0, ctx]
     low_chunks = lax.div(mine + 4, 4)
 
-    def spread_piece(c):
+    def spread(c):
         def step(d):
-            gz(c, d, g_unit(c, d)).wait_recv()
-            for j in (2, 1, 3):
-                gp(c, d, j, 0).start()
-
-        each(1, g_last(c) + 1, step)
-
-    by_core(spread_piece)
-
-    def spread_line(c):
-        def step(d):
-            for j in (1, 2, 3):
-                gp(c, d, j, j).wait_recv()
-            for j in (2, 1, 3):
-                gl(c, d, j, 0).start()
-
-        each(1, g_last(c) + 1, step)
-
-    by_core(spread_line)
+            @pl.when(d <= g_last(c))
+            def _():
+                gz(c, d, g_unit(c, d)).wait_recv()
+                for j in (2, 1, 3):
+                    gp(c, d, j, 0).start()
+
+            e = d - LAG_G
+
+            @pl.when(e >= 1)
+            def _():
+                for j in (1, 2, 3):
+                    gp(c, e, j, j).wait_recv()
+                for j in (2, 1, 3):
+                    gl(c, e, j, 0).start()
+
+        each(1, g_last(c) + LAG_G + 1, step)
+
+    by_core(spread)
 
     def first_keys(t):
         low = keys[wrap(z - t, NZ), 0:2].reshape(CHUNK // 2, CAT)
@@ -378,7 +409,8 @@
 
     def rz(c, k):
         unit = r_unit(c, k)
-        return remote(terms.at[unit, x, y], ring_in.at[k], rz_s.at[k], rz_r.at[k], at_z(unit))
+        device = {"ctx": unit * 2 + holder, "head": head}
+        return remote(terms.at[unit, x, y], ring_in.at[c, k], rz_s.at[k], rz_r.at[c, k], device)
 
     def first_grads(k):
         n = k - 1
@@ -452,100 +484,102 @@
     for store in stores:
         store.start()
 
-    def sum_lines(c):
+    def sum_line(c, k):
+        unit = r_unit(c, k)
+        for j in (1, 2, 3):
+            rl(c, k, j).wait_recv()
+        total = terms[unit, :, y] if c == 0 else terms[unit, x]
+        total = total.astype(f32)
+        for j in range(3):
+            total = total + line_in[k, j].astype(f32)
+        if c == 0:
+            terms[unit, :, y] = total.astype(bf16)
+        else:
+            terms[unit, x] = total.astype(bf16)
+        for j in (2, 1, 3):
+            rp(c, k, j).start()
+
+    def sum_piece(c, k):
+        unit = r_unit(c, k)
+        for j in (1, 2, 3):
+            rp(c, k, j).wait_recv()
+        total = terms[unit, x, y].astype(f32)
+        for j in range(3):
+            total = total + piece_in[k, j].astype(f32)
+        terms[unit, x, y] = total.astype(bf16)
+
+        if c == 0:
+            rz(c, k).start()
+        else:
+            kept = (k == 0) & holds
+
+            @pl.when(kept)
+            def _():
+                ring_in[c, 0] = terms[unit, x, y]
+
+            @pl.when(jnp.logical_not(kept))
+            def _():
+                rz(c, k).start()
+
+    def sum_over_plane(c):
         def step(i):
             k = HALF - i
 
             @pl.when((k >= r_end(c)) & (k <= r_first(c)))
             def _():
-                unit = r_unit(c, k)
-                for j in (1, 2, 3):
-                    rl(c, k, j).wait_recv()
-                total = terms[unit, :, y] if c == 0 else terms[unit, x]
-                total = total.astype(f32)
-                for j in range(3):
-                    total = total + line_in[k, j].astype(f32)
-                if c == 0:
-                    terms[unit, :, y] = total.astype(bf16)
-                else:
-                    terms[unit, x] = total.astype(bf16)
-                for j in (2, 1, 3):
-                    rp(c, k, j).start()
-
-        each(0, HALF + 1, step)
-
-    by_core(sum_lines)
-
-    def sum_pieces(c):
-        def step(i):
-            k = HALF - i
-
-            @pl.when((k >= r_end(c)) & (k <= r_first(c)))
-            def _():
-                unit = r_unit(c, k)
-                for j in (1, 2, 3):
-                    rp(c, k, j).wait_recv()
-                total = terms[unit, x, y].astype(f32)
-                for j in range(3):
-                    total = total + piece_in[k, j].astype(f32)
-                terms[unit, x, y] = total.astype(bf16)
-
-                @pl.when(k >= 1)
-                def _():
-                    rz(c, k).start()
-
-        each(0, HALF + 1, step)
-
-    by_core(sum_pieces)
-
-    def sum_ring(c):
-        share[...] = jnp.zeros((PIECE, CAT), f32) if c == 0 else terms[z, x, y].astype(f32)
-
-        def step(k):
-            rz(c, k).wait_recv()
-            share[...] += ring_in[k].astype(f32)
-
-        each(1, r_first(c) + 1, step)
-
-    by_core(sum_ring)
-
-    holds = lax.rem(x, 2) == core
-    half_of = lax.div(x, 2)
-
-    def rh():
-        return remote(share, share_in, rh_s.at[0], rh_r.at[0], sibling)
-
-    def f1(j, back):
-        ref = final.at[wrap(y - back, NP)]
-        return remote(ref, ref, f1_s.at[j], f1_r.at[j], at_y(j))
-
-    def f2(j, back):
-        ref = result.at[lax.div(wrap(x - back, NP), 2)]
-        return remote(final, ref, f2_s.at[j], f2_r.at[j], at_x(j))
+                sum_line(c, k)
+
+            late = k + LAG_R
+
+            @pl.when((late >= r_end(c)) & (late <= r_first(c)))
+            def _():
+                sum_piece(c, late)
+
+        each(0, HALF + 1 + LAG_R, step)
+
+    by_core(sum_over_plane)
+
+    def f1(i, j, back):
+        if back:
+            xs, ys = wrap(x - i, NP), wrap(y - j, NP)
+        else:
+            xs, ys = x, y
+        ref = result.at[lax.div(xs, 2), ys]
+        return remote(ref, ref, f1_s.at[i, j], f1_r.at[i, j], at_plane(i, j))
+
+    far_first = sorted(
+        ((i, j) for i in range(NP) for j in range(NP) if i or j),
+        key=lambda ij: -(min(ij[0], NP - ij[0]) + min(ij[1], NP - ij[1])),
+    )
 
     @pl.when(holds)
     def _():
-        rh().wait_recv()
-        final[y] = (share[...] + share_in[...]).astype(bf16)
-        for j in (2, 1, 3):
-            f1(j, 0).start()
-        for j in (1, 2, 3):
-            f1(j, j).wait_recv()
-        for j in (2, 1, 3):
-            f2(j, 0).start()
-        result[half_of] = final[...]
-
-    @pl.when(jnp.logical_not(holds))
-    def _():
-        rh().start()
-
-    for j in (1, 2, 3):
-
-        @pl.when(lax.rem(x + NP - j, 2) == core)
+        share[...] = jnp.zeros((PIECE, CAT), f32)
+        for c in range(2):
+
+            def step(i, c=c):
+                k = HALF - i
+
+                @pl.when((k >= r_end(c)) & (k <= r_first(c)))
+                def _():
+                    @pl.when(jnp.logical_not((k == 0) & (core == 1)))
+                    def _():
+                        rz(c, k).wait_recv()
+
+                    share[...] += ring_in[c, k].astype(f32)
+
+            each(0, HALF + 1, step)
+        result[lax.div(x, 2), y] = share[...].astype(bf16)
+        for i, j in far_first:
+            f1(i, j, False).start()
+
+    for i, j in reversed(far_first):
+
+        @pl.when(lax.rem(x + NP - i, 2) == core)
         def _():
-            f2(j, j).wait_recv()
-
-    gain_row = gain[...].astype(f32)
+            f1(i, j, True).wait_recv()
+
+    gain_row = gain[...].reshape(1, LAT).astype(f32)
     kv_rows = kv_t[...].T
     grads = result[...].reshape(2 * SPAN, CAT).astype(f32)
     values = kv_rows[:, :LAT].astype(f32)
@@ -583,31 +617,37 @@
 
         each(r_end(c), r_first(c) + 1, reduce_step)
         each(1, r_first(c) + 1, lambda k: rz(c, k).wait_send())
+        if c == 1:
+
+            @pl.when(jnp.logical_not(holds))
+            def _():
+                rz(c, 0).wait_send()
 
     by_core(sends)
 
     @pl.when(holds)
     def _():
-        for j in (1, 2, 3):
-            f1(j, 0).wait_send()
-            f2(j, 0).wait_send()
-
-    @pl.when(jnp.logical_not(holds))
-    def _():
-        rh().wait_send()
+        for i, j in far_first:
+            f1(i, j, False).wait_send()
 
     for done in stores:
         done.wait()
     store.wait()
+
+
+def hand_over(*refs):
+    for src, dst in zip(refs[:3], refs[3:]):
+        dst[...] = src[...]
 
 
 def local(q_nope, q_rope, kv_cache, kv_gain, w_uk, w_uv, attn_out, d_out, span_table):
     toks = q_nope.shape[0]
     hbm = pl.BlockSpec(memory_space=pl.ANY)
     smem = pl.BlockSpec(memory_space=pltpu.SMEM)
+    vmem = pl.BlockSpec(memory_space=pltpu.VMEM)
     dma = pltpu.SemaphoreType.DMA
     inputs = (
-        q_nope, q_rope, kv_cache.T, kv_gain.reshape(1, LAT), w_uk, w_uv, attn_out, d_out
+        q_nope, q_rope, kv_cache.T, kv_gain, w_uk, w_uv, attn_out, d_out
     )
     out_shape = (
         jax.ShapeDtypeStruct((toks, HEADS * NOPE), bf16),
@@ -622,10 +662,8 @@
         pltpu.VMEM((HALF + 1, NP, NP, PIECE, CAT), bf16),
         pltpu.VMEM((HALF + 1, 3, NP, PIECE, CAT), bf16),
         pltpu.VMEM((HALF + 1, 3, PIECE, CAT), bf16),
-        pltpu.VMEM((HALF + 1, PIECE, CAT), bf16),
+        pltpu.VMEM((2, HALF + 1, PIECE, CAT), bf16),
         pltpu.VMEM((PIECE, CAT), f32),
-        pltpu.VMEM((PIECE, CAT), f32),
-        pltpu.VMEM((NP, PIECE, CAT), bf16),
         pltpu.VMEM((2, NP, PIECE, CAT), bf16),
         pltpu.VMEM((2, ROWS, CAT), bf16),
         pltpu.VMEM((2, ROWS, LAT), bf16),
@@ -649,12 +687,10 @@
         dma((HALF + 1,)), dma((HALF + 1,)),
         dma((HALF + 1, NP)), dma((HALF + 1, NP)),
         dma((HALF + 1, NP)), dma((HALF + 1, NP)),
-        dma((HALF + 1,)), dma((HALF + 1,)),
-        dma((1,)), dma((1,)),
-        dma((NP,)), dma((NP,)),
-        dma((NP,)), dma((NP,)),
+        dma((HALF + 1,)), dma((2, HALF + 1)),
+        dma((NP, NP)), dma((NP, NP)),
     ]
-    d_q_nope, d_q_rope, d_cache = pl.pallas_call(
+    results = pl.pallas_call(
         kernel,
         out_shape=out_shape,
         in_specs=[hbm] * len(inputs) + [smem],
@@ -664,6 +700,13 @@
             collective_id=0, has_side_effects=True, vmem_limit_bytes=60 * 1024 * 1024
         ),
     )(*inputs, span_table.T)
+    d_q_nope, d_q_rope, d_cache = pl.pallas_call(
+        hand_over,
+        out_shape=out_shape,
+        in_specs=[vmem] * 3,
+        out_specs=(vmem, vmem, vmem),
+        compiler_params=pltpu.CompilerParams(vmem_limit_bytes=60 * 1024 * 1024),
+    )(*results)
     return d_q_nope, d_q_rope, d_cache.T
 
 

time: 108 us -> 94.2 us (0.87)
  Pallas kernels: 102 us -> 93.4 us
  local copies, waits for them, and re-layouts: 5.05 us -> 0 us
    pallas_call x1, Pallas kernels: 102 us -> 91.6 us  [local(): pl.pallas_call(kernel, out_shape=out_shape, in_specs=[hbm] * len(inputs)...]
    unnamed x7 -> x0, local copies, waits for them, and re-layouts: 4.47 us -> none
    pallas_call x0 -> x1, Pallas kernels: none -> 1.85 us  [local(): pl.pallas_call(hand_over, out_shape=out_shape, in_specs=[vmem] * 3, out_s...]
where the time goes in v3:
time: 94.2 us; the launch traced here: 94.1 us
  Pallas kernels  93.4 us (99%)
    pallas_call x1, Pallas kernels, local(): pl.pallas_call(kernel, out_shape=out_shape, in_specs=[hbm] * len(inputs)...  91.6 us

profile of v3, /device:TPU:1, one launch (start us, length us, event | category | flops | bytes accessed | tf_op | source)
XLA Modules:
  0.0 94.1 jit_solution(13742739767196846438)
XLA Ops:
  0.6 91.6 %shard_map.112 = (bf16[128,512]{1,0:T(8,128)(2,1)}, bf16[128,256]{1,0:T(8,128)(2,1)}, f32[576,128]{1,0:T(8,128)}) custom-call(bf16[128,512]{1,0:T(8,128)(2,1)} %q_nope_in.1, bf16[128,256]{1,0:T(8,128)(2,1)} %q_rope_in.1, bf16[576,128]{1,0:T(8,128)(2,1)} %bitcast.3, bf16[512]{0:T(512)(128)(2,1)} %gain_in.1, bf16[4,128,512]{2,1,0:T(8,128)(2,1)} %w_uk_in.1, ...), custom_call_target="tpu_custom_call" | custom-call | tf_op jit(solution)/shard_map/pallas_call | solution.py:693
  92.2 1.8 %shard_map.113 = (bf16[128,512]{1,0:T(8,128)(2,1)}, bf16[128,256]{1,0:T(8,128)(2,1)}, f32[576,128]{1,0:T(8,128)}) custom-call(bf16[128,512]{1,0:T(8,128)(2,1)} %get-tuple-element.9.refs_0_, bf16[128,256]{1,0:T(8,128)(2,1)} %get-tuple-element.10.refs_1_, f32[576,128]{1,0:T(8,128)} %get-tuple-element.11.refs_2_), custom_call_target="tpu_custom_call" | custom-call | tf_op jit(solution)/shard_map/pallas_call | solution.py:703

commit v4 on v3

--- a/solution.py
+++ b/solution.py
@@ -22,12 +22,15 @@
 LAT = 512
 ROPE = 64
 LAG_G = 4
+NEAR = 2
 LAG_R = 2
 CAT = LAT + ROPE
 NOPE = 128
 CHUNK = 256
 FIRST = 8
 OTHER = 9
+OWN_LOW = 2 * NZ
+HIDDEN = OWN_LOW + 1
 BLANK = 4 * OTHER
 
 f32 = jnp.float32
@@ -47,11 +50,11 @@
     dq_nope_res, dq_rope_res, d_cache_res,
     q_nope, q_rope, kv_t, gain, w_uk, w_uv, attn_out, d_out,
     dq_nope_out, dq_rope_out, d_cache_out,
-    keys, terms, sib_in, line_in, piece_in, ring_in, share, result,
-    queries, d_latent, delta, scores, d_prob, tops, other_terms, dq_prefix, dq_first,
+    keys, terms, sib_in, line_in, piece_in, ring_in, whole_in, share, result,
+    queries, d_latent, delta, scores, d_prob, other_scores, other_prob, tops, other_terms, dq_prefix, dq_first,
     stats, sums, inverse, in_sem, out_sem,
     g0_s, g0_r, gz_s, gz_r, gp_s, gp_r, gl_s, gl_r, gs_s, gs_r,
-    ra_s, ra_r, rl_s, rl_r, rp_s, rp_r, rz_s, rz_r, f1_s, f1_r,
+    ra_s, ra_r, rl_s, rl_r, rp_s, rp_r, rz_s, rz_r, rw_s, rw_r, f1_s, f1_r,
 ):
     scale = float(NOPE + ROPE) ** (-0.5)
     ctx = lax.axis_index("ctx")
@@ -95,10 +98,12 @@
     def greet(c):
         for d in range(HALF if c == 0 else HALF - 1, 0, -1):
             signal({"ctx": wrap(z - d if c == 0 else z + d, NZ) * 2 + c, "head": head})
+        if c == 1:
+            signal({"ctx": wrap(z - 1, NZ) * 2, "head": head})
 
         @pl.when(holds)
         def _():
-            for d in range(HALF - 1 if c == 0 else HALF, 0, -1):
+            for d in range(HALF - 1 if c == 0 else HALF, 1, -1):
                 signal({"ctx": wrap(z + d if c == 0 else z - d, NZ) * 2 + 1 - c, "head": head})
 
     by_core(greet)
@@ -163,10 +168,13 @@
     tops[...] = jnp.full(tops.shape, NEG_BIG, f32)
     dq_first[...] = jnp.zeros(dq_first.shape, f32)
     other_terms[BLANK] = jnp.zeros((SPAN, CAT), f32)
-
-    z_targets = HALF - core
-    targets = 2 * (NP - 1) + 1 + z_targets
-    pl.semaphore_wait(barrier, jnp.where(holds, targets + (NP - 1) ** 2, targets + z_targets))
+    other_scores[HIDDEN] = jnp.full((SPAN, ROWS), NEG_BIG, f32)
+    other_prob[HIDDEN] = jnp.zeros((SPAN, ROWS), f32)
+
+    targets = 2 * (NP - 1) + 1
+    held = targets + (NP - 1) ** 2 + (HALF + 1) - 2 * core
+    given = targets + 2 * HALF - 3 * core
+    pl.semaphore_wait(barrier, jnp.where(holds, held, given))
 
     def g_last(c):
         return HALF if c == 0 else HALF - 1
@@ -182,8 +190,13 @@
         ref = keys.at[z, 2 * n + twin]
         return remote(ref, ref, g0_s.at[n], g0_r.at[n], sibling)
 
-    def gz(c, d, unit):
-        ref = keys.at[unit, x, y]
+    def gz(c, d, unit, form="piece"):
+        if form == "unit":
+            ref = keys.at[unit]
+        elif form == "line":
+            ref = keys.at[unit, :, y] if c == 0 else keys.at[unit, x]
+        else:
+            ref = keys.at[unit, x, y]
         device = at_z(wrap(z + d, NZ) if c == 0 else wrap(z - d, NZ))
         return remote(ref, ref, gz_s.at[d], gz_r.at[d], device)
 
@@ -220,7 +233,9 @@
         lax.fori_loop(low, high, body, 0)
 
     def spread_z(c):
-        each(1, g_last(c) + 1, lambda d: gz(c, d, z).start())
+        each(NEAR + 1, g_last(c) + 1, lambda d: gz(c, g_last(c) + NEAR + 1 - d, z).start())
+        each(2, NEAR + 1, lambda d: gz(c, d, z, "line").start())
+        gz(c, 1, z, "unit").start()
 
     by_core(spread_z)
 
@@ -236,6 +251,13 @@
     low_chunks = lax.div(mine + 4, 4)
 
     def spread(c):
+        def near_step(d):
+            gz(c, d, g_unit(c, d), "line").wait_recv()
+            for j in (2, 1, 3):
+                gl(c, d, j, 0).start()
+
+        each(2, NEAR + 1, near_step)
+
         def step(d):
             @pl.when(d <= g_last(c))
             def _():
@@ -245,14 +267,14 @@
 
             e = d - LAG_G
 
-            @pl.when(e >= 1)
+            @pl.when(e >= NEAR + 1)
             def _():
                 for j in (1, 2, 3):
                     gp(c, e, j, j).wait_recv()
                 for j in (2, 1, 3):
                     gl(c, e, j, 0).start()
 
-        each(1, g_last(c) + LAG_G + 1, step)
+        each(NEAR + 1, g_last(c) + LAG_G + 1, step)
 
     by_core(spread)
 
@@ -267,12 +289,28 @@
             part = op(part, value[r : r + 8])
         return part
 
+    key_in = lax.broadcasted_iota(jnp.int32, (SPAN, ROWS), 0)
+    tok_in = lax.rem(lax.broadcasted_iota(jnp.int32, (SPAN, ROWS), 1), SPAN)
+
+    own_low = keys[z, core].reshape(SPAN, CAT)
+    own_part = jnp.where(key_in <= tok_in, dot(own_low, queries[0], 1, 1), NEG_BIG)
+    other_scores[OWN_LOW] = own_part
+    other_prob[OWN_LOW] = dot(own_low[:, :LAT], d_latent[0], 1, 1)
+    tops[0] = fold_rows(own_part, jnp.maximum)
+
     def arrivals(d):
         def own(c):
-            @pl.when(d <= g_last(c))
+            @pl.when(d == 1)
+            def _():
+                gz(c, 1, g_unit(c, 1), "unit").wait_recv()
+
+            @pl.when((d >= 2) & (d <= g_last(c)))
             def _():
                 for j in (1, 2, 3):
                     gl(c, d, j, j).wait_recv()
+
+            @pl.when(d <= g_last(c))
+            def _():
                 gs(c, d).start()
 
             @pl.when((d >= 2) & (d - 1 <= g_last(1 - c)))
@@ -287,8 +325,32 @@
             chunk = first_keys(t)
             part = dot(chunk, queries[1], 1, 1)
             scores[t - 1] = part
-            tops[OTHER] = jnp.maximum(tops[OTHER], fold_rows(part, jnp.maximum))
+            tops[1] = jnp.maximum(tops[1], fold_rows(part, jnp.maximum))
             d_prob[t - 1] = dot(chunk[:, :LAT], d_latent[1], 1, 1)
+
+            slots, kinds, blocks = [], [], []
+            for unit in (wrap(z - t, NZ), wrap(z + lax.rem(t, HALF), NZ)):
+                for cc in range(2):
+                    slot = unit * 2 + cc
+                    kind = jnp.where(table[0, slot] >= mine, 1, 0)
+                    slots.append(slot)
+                    kinds.append(kind)
+                    block = jnp.where(kind == 1, keys[unit, 2 + cc], keys[unit, cc])
+                    blocks.append(block.reshape(SPAN, CAT))
+            chunk = jnp.concatenate(blocks, axis=0)
+            part = [dot(chunk, queries[kind], 1, 1) for kind in range(2)]
+            d_part = [dot(chunk[:, :LAT], d_latent[kind], 1, 1) for kind in range(2)]
+            for n in range(4):
+                rows = slice(n * SPAN, (n + 1) * SPAN)
+                high = kinds[n] == 1
+                block = jnp.where(high, part[1][rows], part[0][rows])
+                gap = jnp.where(slots[n] == ctx, 0, -SPAN)
+                block = jnp.where(key_in + gap <= tok_in, block, NEG_BIG)
+                other_scores[slots[n]] = block
+                other_prob[slots[n]] = jnp.where(high, d_part[1][rows], d_part[0][rows])
+                top = fold_rows(block, jnp.maximum)
+                tops[0] = jnp.maximum(tops[0], jnp.where(high, NEG_BIG, top))
+                tops[1] = jnp.maximum(tops[1], jnp.where(high, top, NEG_BIG))
 
     each(1, HALF + 2, arrivals)
 
@@ -306,42 +368,39 @@
             blocks.append(block.reshape(SPAN, CAT))
         return jnp.concatenate(blocks, axis=0)
 
-    key_in = lax.broadcasted_iota(jnp.int32, (CHUNK, ROWS), 0)
-    tok_in = lax.rem(lax.broadcasted_iota(jnp.int32, (CHUNK, ROWS), 1), SPAN)
-
-    def other_scores(j, carry):
-        kind = kind_of(j)
-        chunk = other_keys(j)
-        low_gap = (4 * j - mine) * SPAN
-        high_gap = (4 * (j - low_chunks) - (2 * NZ - 1 - mine)) * SPAN
-        gap = jnp.where(kind == 1, high_gap, low_gap)
-        part = dot(chunk, queries[kind], 1, 1)
-        part = jnp.where(key_in + gap <= tok_in, part, NEG_BIG)
-        scores[FIRST + j] = part
-        tops[j] = fold_rows(part, jnp.maximum)
-        d_prob[FIRST + j] = dot(chunk[:, :LAT], d_latent[kind], 1, 1)
-        return carry
-
-    lax.fori_loop(0, OTHER, other_scores, 0)
-
-    top_low = jnp.full((8, ROWS), NEG_BIG, f32)
-    top_high = tops[OTHER]
-    for j in range(OTHER):
-        high = j >= low_chunks
-        top_low = jnp.maximum(top_low, jnp.where(high, NEG_BIG, tops[j]))
-        top_high = jnp.maximum(top_high, jnp.where(high, tops[j], NEG_BIG))
+    def other_slots(j):
+        slots = []
+        for i in range(4):
+            low = 4 * j + i
+            low_slot = inverse[jnp.minimum(low, 2 * NZ - 1)]
+            low_slot = jnp.where(low < mine, low_slot, jnp.where(low == mine, OWN_LOW, HIDDEN))
+            high = 2 * NZ - 1 - (4 * (j - low_chunks) + i)
+            high_slot = inverse[jnp.clip(high, 0, 2 * NZ - 1)]
+            high_slot = jnp.where(high >= mine, high_slot, HIDDEN)
+            slots.append(jnp.where(j >= low_chunks, high_slot, low_slot))
+        return slots
+
+    top_low, top_high = tops[0], tops[1]
     rate = scale * LOG2_E
     stats[0] = jnp.max(top_low, axis=0, keepdims=True) * rate
     stats[1] = jnp.max(top_high, axis=0, keepdims=True) * rate
 
     def exponents(n, carry):
-        kind = jnp.where(n < FIRST, 1, kind_of(n - FIRST))
-        part = jnp.exp2(scores[n] * rate - stats[kind])
+        part = jnp.exp2(scores[n] * rate - stats[1])
         scores[n] = part
         sums[n] = fold_rows(part, jnp.add)
         return carry
 
-    lax.fori_loop(0, FIRST + OTHER, exponents, 0)
+    lax.fori_loop(0, FIRST, exponents, 0)
+
+    def other_exponents(j, carry):
+        value = jnp.concatenate([other_scores[slot] for slot in other_slots(j)], axis=0)
+        part = jnp.exp2(value * rate - stats[kind_of(j)])
+        scores[FIRST + j] = part
+        sums[FIRST + j] = fold_rows(part, jnp.add)
+        return carry
+
+    lax.fori_loop(0, OTHER, other_exponents, 0)
 
     sum_low = jnp.zeros((8, ROWS), f32)
     sum_high = jnp.zeros((8, ROWS), f32)
@@ -354,18 +413,19 @@
     stats[0] = 1.0 / jnp.sum(sum_low, axis=0, keepdims=True)
     stats[1] = 1.0 / jnp.sum(sum_high, axis=0, keepdims=True)
 
-    def chunk_grads(n, kind, chunk):
+    def chunk_grads(n, kind, chunk, d_part):
         expo = scores[n]
         inv_sum = stats[kind]
         prob = (expo * inv_sum).astype(bf16)
-        d_score = ((d_prob[n] - delta[kind]) * (expo * (inv_sum * scale))).astype(bf16)
+        d_score = ((d_part - delta[kind]) * (expo * (inv_sum * scale))).astype(bf16)
         dq = dot(d_score, chunk, 0, 0)
         dk = dot(d_score, queries[kind], 1, 0)
         dk_lat = dk[:, :LAT] + dot(prob, d_latent[kind], 1, 0)
         return dq, dk_lat, dk[:, LAT:]
 
     def other_grads(j, carry):
-        dq, dk_lat, dk_rope = chunk_grads(FIRST + j, kind_of(j), other_keys(j))
+        d_part = jnp.concatenate([other_prob[slot] for slot in other_slots(j)], axis=0)
+        dq, dk_lat, dk_rope = chunk_grads(FIRST + j, kind_of(j), other_keys(j), d_part)
         for i in range(4):
             rows = slice(i * SPAN, (i + 1) * SPAN)
             other_terms[4 * j + i, :, :LAT] = dk_lat[rows]
@@ -412,9 +472,14 @@
         device = {"ctx": unit * 2 + holder, "head": head}
         return remote(terms.at[unit, x, y], ring_in.at[c, k], rz_s.at[k], rz_r.at[c, k], device)
 
+    def rw(c):
+        unit = r_unit(c, 1)
+        device = {"ctx": unit * 2 + 1, "head": head}
+        return remote(terms.at[unit], whole_in.at[c], rw_s.at[0], rw_r.at[c], device)
+
     def first_grads(k):
         n = k - 1
-        dq, dk_lat, dk_rope = chunk_grads(n, 1, first_keys(k))
+        dq, dk_lat, dk_rope = chunk_grads(n, 1, first_keys(k), d_prob[n])
         dq_first[...] += dq
         units = (wrap(z - k, NZ), wrap(z + lax.rem(k, HALF), NZ))
         for s in range(2):
@@ -433,28 +498,56 @@
                 )
                 terms[unit, 2 + cc] = other_terms[high_slot].astype(bf16).reshape(NP, PIECE, CAT)
 
+    def turn(i):
+        return jnp.where(i == 0, 1, jnp.where(i == HALF, 0, HALF + 1 - i))
+
+    def served(c, k):
+        return (k >= r_end(c)) & (k <= r_first(c))
+
     def reduce_step(i):
+        k = turn(i)
+
         @pl.when(i < HALF)
         def _():
-            first_grads(HALF - i)
-
-        k = HALF - i
+            first_grads(k)
 
         def own(c):
-            @pl.when((k >= r_end(1 - c)) & (k <= r_first(1 - c)))
+            @pl.when((i <= HALF) & served(1 - c, k))
             def _():
                 ra(1 - c, k).start()
 
-            ka = k + 1
-
-            @pl.when((ka >= r_end(c)) & (ka <= r_first(c)))
+            ka = turn(i - 1)
+
+            @pl.when((i >= 1) & served(c, ka))
             def _():
                 unit = r_unit(c, ka)
                 ra(c, ka).wait_recv()
                 both = terms[unit].astype(f32) + sib_in[ka].astype(f32)
-                terms[unit] = both.astype(bf16)
-                for j in (2, 1, 3):
-                    rl(c, ka, j).start()
+                if c == 1:
+                    added = ka == 0
+
+                    @pl.when(added)
+                    def _():
+                        rw(0).wait_recv()
+                        rw(1).wait_recv()
+                        total = both + whole_in[0].astype(f32) + whole_in[1].astype(f32)
+                        terms[unit] = total.astype(bf16)
+
+                    @pl.when(jnp.logical_not(added))
+                    def _():
+                        terms[unit] = both.astype(bf16)
+
+                else:
+                    terms[unit] = both.astype(bf16)
+
+                @pl.when(ka == 1)
+                def _():
+                    rw(c).start()
+
+                @pl.when(ka != 1)
+                def _():
+                    for j in (2, 1, 3):
+                        rl(c, ka, j).start()
 
         by_core(own)
 
@@ -521,21 +614,24 @@
             def _():
                 rz(c, k).start()
 
+    def plane_turn(i):
+        return jnp.where(i == HALF - 1, 0, HALF - i)
+
     def sum_over_plane(c):
         def step(i):
-            k = HALF - i
-
-            @pl.when((k >= r_end(c)) & (k <= r_first(c)))
+            k = plane_turn(i)
+
+            @pl.when((i < HALF) & served(c, k))
             def _():
                 sum_line(c, k)
 
-            late = k + LAG_R
-
-            @pl.when((late >= r_end(c)) & (late <= r_first(c)))
+            late = plane_turn(i - LAG_R)
+
+            @pl.when((i >= LAG_R) & served(c, late))
             def _():
                 sum_piece(c, late)
 
-        each(0, HALF + 1 + LAG_R, step)
+        each(0, HALF + LAG_R, step)
 
     by_core(sum_over_plane)
 
@@ -558,9 +654,9 @@
         for c in range(2):
 
             def step(i, c=c):
-                k = HALF - i
-
-                @pl.when((k >= r_end(c)) & (k <= r_first(c)))
+                k = plane_turn(i)
+
+                @pl.when(served(c, k))
                 def _():
                     @pl.when(jnp.logical_not((k == 0) & (core == 1)))
                     def _():
@@ -568,7 +664,7 @@
 
                     share[...] += ring_in[c, k].astype(f32)
 
-            each(0, HALF + 1, step)
+            each(0, HALF, step)
         result[lax.div(x, 2), y] = share[...].astype(bf16)
         for i, j in far_first:
             f1(i, j, False).start()
@@ -597,26 +693,40 @@
 
     def sends(c):
         def gather_step(d):
-            gz(c, d, z).wait_send()
+            @pl.when(d <= NEAR)
+            def _():
+                gz(c, d, z, "line").wait_send()
+
+            @pl.when(d > NEAR)
+            def _():
+                gz(c, d, z).wait_send()
+                for j in (1, 2, 3):
+                    gp(c, d, j, 0).wait_send()
+
             for j in (1, 2, 3):
-                gp(c, d, j, 0).wait_send()
                 gl(c, d, j, 0).wait_send()
             gs(c, d).wait_send()
 
-        each(1, g_last(c) + 1, gather_step)
+        gz(c, 1, z, "unit").wait_send()
+        gs(c, 1).wait_send()
+
+        each(2, g_last(c) + 1, gather_step)
 
         def reduce_twin(k):
             ra(1 - c, k).wait_send()
 
         each(r_end(1 - c), r_first(1 - c) + 1, reduce_twin)
 
-        def reduce_step(k):
+        def reduce_sends(k):
             for j in (1, 2, 3):
                 rl(c, k, j).wait_send()
                 rp(c, k, j).wait_send()
 
-        each(r_end(c), r_first(c) + 1, reduce_step)
-        each(1, r_first(c) + 1, lambda k: rz(c, k).wait_send())
+        rw(c).wait_send()
+        if c == 1:
+            reduce_sends(0)
+        each(2, r_first(c) + 1, reduce_sends)
+        each(2, r_first(c) + 1, lambda k: rz(c, k).wait_send())
         if c == 1:
 
             @pl.when(jnp.logical_not(holds))
@@ -663,14 +773,17 @@
         pltpu.VMEM((HALF + 1, 3, NP, PIECE, CAT), bf16),
         pltpu.VMEM((HALF + 1, 3, PIECE, CAT), bf16),
         pltpu.VMEM((2, HALF + 1, PIECE, CAT), bf16),
+        pltpu.VMEM((2, NP, NP, PIECE, CAT), bf16),
         pltpu.VMEM((PIECE, CAT), f32),
         pltpu.VMEM((2, NP, PIECE, CAT), bf16),
         pltpu.VMEM((2, ROWS, CAT), bf16),
         pltpu.VMEM((2, ROWS, LAT), bf16),
         pltpu.VMEM((2, 1, ROWS), f32),
         pltpu.VMEM((FIRST + OTHER, CHUNK, ROWS), f32),
-        pltpu.VMEM((FIRST + OTHER, CHUNK, ROWS), f32),
-        pltpu.VMEM((OTHER + 1, 8, ROWS), f32),
+        pltpu.VMEM((FIRST, CHUNK, ROWS), f32),
+        pltpu.VMEM((HIDDEN + 1, SPAN, ROWS), f32),
+        pltpu.VMEM((HIDDEN + 1, SPAN, ROWS), f32),
+        pltpu.VMEM((2, 8, ROWS), f32),
         pltpu.VMEM((BLANK + 1, SPAN, CAT), f32),
         pltpu.VMEM((OTHER, ROWS, CAT), f32),
         pltpu.VMEM((ROWS, CAT), f32),
@@ -688,6 +801,7 @@
         dma((HALF + 1, NP)), dma((HALF + 1, NP)),
         dma((HALF + 1, NP)), dma((HALF + 1, NP)),
         dma((HALF + 1,)), dma((2, HALF + 1)),
+        dma((1,)), dma((2,)),
         dma((NP, NP)), dma((NP, NP)),
     ]
     results = pl.pallas_call(

time: 94.2 us -> 92 us (0.977)
  Pallas kernels: 93.4 us -> 91.1 us
    pallas_call x1, Pallas kernels: 91.6 us -> 89.3 us  [local(): pl.pallas_call(kernel, out_shape=out_shape, in_specs=[hbm] * len(inputs)...]
where the time goes in v4:
time: 92 us; the launch traced here: 91.8 us
  Pallas kernels  91.1 us (99%)
    pallas_call x1, Pallas kernels, local(): pl.pallas_call(kernel, out_shape=out_shape, in_specs=[hbm] * len(inputs)...  89.3 us
    pallas_call x1, Pallas kernels, local(): pl.pallas_call(hand_over, out_shape=out_shape, in_specs=[vmem] * 3, out_s...  1.85 us

profile of v4, /device:TPU:1, one launch (start us, length us, event | category | flops | bytes accessed | tf_op | source)
XLA Modules:
  0.0 91.8 jit_solution(10715200016583151964)
XLA Ops:
  0.6 89.3 %shard_map.112 = (bf16[128,512]{1,0:T(8,128)(2,1)}, bf16[128,256]{1,0:T(8,128)(2,1)}, f32[576,128]{1,0:T(8,128)}) custom-call(bf16[128,512]{1,0:T(8,128)(2,1)} %q_nope_in.1, bf16[128,256]{1,0:T(8,128)(2,1)} %q_rope_in.1, bf16[576,128]{1,0:T(8,128)(2,1)} %bitcast.3, bf16[512]{0:T(512)(128)(2,1)} %gain_in.1, bf16[4,128,512]{2,1,0:T(8,128)(2,1)} %w_uk_in.1, ...), custom_call_target="tpu_custom_call" | custom-call | tf_op jit(solution)/shard_map/pallas_call | solution.py:807
  89.9 1.8 %shard_map.113 = (bf16[128,512]{1,0:T(8,128)(2,1)}, bf16[128,256]{1,0:T(8,128)(2,1)}, f32[576,128]{1,0:T(8,128)}) custom-call(bf16[128,512]{1,0:T(8,128)(2,1)} %get-tuple-element.9.refs_0_, bf16[128,256]{1,0:T(8,128)(2,1)} %get-tuple-element.10.refs_1_, f32[576,128]{1,0:T(8,128)} %get-tuple-element.11.refs_2_), custom_call_target="tpu_custom_call" | custom-call | tf_op jit(solution)/shard_map/pallas_call | solution.py:817

commit v5 on v4

--- a/solution.py
+++ b/solution.py
@@ -52,7 +52,7 @@
     dq_nope_out, dq_rope_out, d_cache_out,
     keys, terms, sib_in, line_in, piece_in, ring_in, whole_in, share, result,
     queries, d_latent, delta, scores, d_prob, other_scores, other_prob, tops, other_terms, dq_prefix, dq_first,
-    stats, sums, inverse, in_sem, out_sem,
+    stats, sums, values_ref, inv_ref, inverse, in_sem, out_sem,
     g0_s, g0_r, gz_s, gz_r, gp_s, gp_r, gl_s, gl_r, gs_s, gs_r,
     ra_s, ra_r, rl_s, rl_r, rp_s, rp_r, rz_s, rz_r, rw_s, rw_r, f1_s, f1_r,
 ):
@@ -499,7 +499,8 @@
                 terms[unit, 2 + cc] = other_terms[high_slot].astype(bf16).reshape(NP, PIECE, CAT)
 
     def turn(i):
-        return jnp.where(i == 0, 1, jnp.where(i == HALF, 0, HALF + 1 - i))
+        later = jnp.where(i == HALF, 0, HALF + 1 - i)
+        return jnp.where(i == 0, HALF, jnp.where(i == 1, 1, later))
 
     def served(c, k):
         return (k >= r_end(c)) & (k <= r_first(c))
@@ -577,6 +578,11 @@
     for store in stores:
         store.start()
 
+    gain_row = gain[...].reshape(1, LAT).astype(f32)
+    own_rows = kv_t[...].T[:, :LAT].astype(f32)
+    values_ref[...] = own_rows
+    inv_ref[...] = lax.rsqrt(jnp.mean(own_rows * own_rows, axis=-1, keepdims=True) + EPS_NORM)
+
     def sum_line(c, k):
         unit = r_unit(c, k)
         for j in (1, 2, 3):
@@ -675,11 +681,9 @@
         def _():
             f1(i, j, True).wait_recv()
 
-    gain_row = gain[...].reshape(1, LAT).astype(f32)
-    kv_rows = kv_t[...].T
     grads = result[...].reshape(2 * SPAN, CAT).astype(f32)
-    values = kv_rows[:, :LAT].astype(f32)
-    inv = lax.rsqrt(jnp.mean(values * values, axis=-1, keepdims=True) + EPS_NORM)
+    values = values_ref[...]
+    inv = inv_ref[...]
     scaled = grads[:, :LAT] * gain_row
     inner = jnp.mean(values * scaled, axis=-1, keepdims=True)
     d_raw = inv * scaled - values * (inv * inv * inv * inner)
@@ -789,6 +793,8 @@
         pltpu.VMEM((ROWS, CAT), f32),
         pltpu.VMEM((2, 1, ROWS), f32),
         pltpu.VMEM((FIRST + OTHER, 8, ROWS), f32),
+        pltpu.VMEM((2 * SPAN, LAT), f32),
+        pltpu.VMEM((2 * SPAN, 1), f32),
         pltpu.SMEM((2 * NZ,), jnp.int32),
         dma((len(inputs),)),
         dma((3,)),

time: 92 us -> 92 us (level)
  no operation moved by 1% of the time
where the time goes in v5:
time: 92 us; the launch traced here: 91.8 us
  Pallas kernels  91.1 us (99%)
    pallas_call x1, Pallas kernels, local(): pl.pallas_call(kernel, out_shape=out_shape, in_specs=[hbm] * len(inputs)...  89.3 us
    pallas_call x1, Pallas kernels, local(): pl.pallas_call(hand_over, out_shape=out_shape, in_specs=[vmem] * 3, out_s...  1.85 us

profile of v5, /device:TPU:1, one launch (start us, length us, event | category | flops | bytes accessed | tf_op | source)
XLA Modules:
  0.0 91.8 jit_solution(13408692307174565107)
XLA Ops:
  0.6 89.3 %shard_map.112 = (bf16[128,512]{1,0:T(8,128)(2,1)}, bf16[128,256]{1,0:T(8,128)(2,1)}, f32[576,128]{1,0:T(8,128)}) custom-call(bf16[128,512]{1,0:T(8,128)(2,1)} %q_nope_in.1, bf16[128,256]{1,0:T(8,128)(2,1)} %q_rope_in.1, bf16[576,128]{1,0:T(8,128)(2,1)} %bitcast.3, bf16[512]{0:T(512)(128)(2,1)} %gain_in.1, bf16[4,128,512]{2,1,0:T(8,128)(2,1)} %w_uk_in.1, ...), custom_call_target="tpu_custom_call" | custom-call | tf_op jit(solution)/shard_map/pallas_call | solution.py:813
  89.9 1.8 %shard_map.113 = (bf16[128,512]{1,0:T(8,128)(2,1)}, bf16[128,256]{1,0:T(8,128)(2,1)}, f32[576,128]{1,0:T(8,128)}) custom-call(bf16[128,512]{1,0:T(8,128)(2,1)} %get-tuple-element.9.refs_0_, bf16[128,256]{1,0:T(8,128)(2,1)} %get-tuple-element.10.refs_1_, f32[576,128]{1,0:T(8,128)} %get-tuple-element.11.refs_2_), custom_call_target="tpu_custom_call" | custom-call | tf_op jit(solution)/shard_map/pallas_call | solution.py:823
